TPU v7x, 32 devices: a whole 2x2x4 slice. The times are simulated.
32 devices in a mesh: groups: 2 (over y), expert: 4 (over x, core), tensor: 4 (over z).
Axes of the slice: x: 2, y: 2, z: 4, core: 2. Of those that a mesh axis runs over, the one named last changes fastest.
Arguments:
- tokens: bfloat16 [2048, 2048], P(('groups', 'expert')), parts along dimension 0, may hold values from -6 to 6
- route_ids: int32 [2048, 2], P(('groups', 'expert')), parts along dimension 0, may hold values from 0 to 3, all different within a row; in each aligned block of 256 rows (0 to 255, 256 to 511, ...) at most 256 rows name the same one
- route_weights: float32 [2048, 2], P(('groups', 'expert')), parts along dimension 0, may hold values from 0.2 to 1
- modulation: float32 [8, 6144], P(('groups', 'expert')), parts along dimension 0, may hold values from -5 to 5
- partner: int32 [4], replicated, may hold values from 0 to 3, as said below
- w_gate: bfloat16 [4, 2048, 4096], P('expert', None, 'tensor'), may hold values from -0.125 to 0.125
- w_up: bfloat16 [4, 2048, 4096], P('expert', None, 'tensor'), may hold values from -0.125 to 0.125
- w_down: bfloat16 [4, 4096, 2048], P('expert', 'tensor'), may hold values from -0.09375 to 0.09375
- spare_gate: bfloat16 [4, 2048, 4096], P('expert', None, 'tensor'), may hold values from -0.125 to 0.125
- spare_up: bfloat16 [4, 2048, 4096], P('expert', None, 'tensor'), may hold values from -0.125 to 0.125
- spare_down: bfloat16 [4, 4096, 2048], P('expert', 'tensor'), may hold values from -0.09375 to 0.09375
Outputs:
- layer_out: bfloat16 [2048, 2048], P(('groups', 'expert'), 'tensor'), parts along dimension 0
There are 2 independent parts, one for each index of `groups`. A program takes and returns all parts, laid end to end along the dimension named above; an argument that names none is the same for every part. Nothing has to cross between parts.
Inputs may be any that keep to these rules, and one draw needn't show every extreme that they name: `route_ids`: the two ids of a token differ. Within the 256 tokens of one image no expert is named more than 2 * 128 times; in some image some expert is named exactly 2 * 128 times. partner is a permutation of the experts with partner[e] != e for every e.
All inputs are finite; a program needn't handle non-finite values.
Results may differ from a plain program's by a relative error of at most 0.014.
Values may be sent and summed in bfloat16 or wider, within the bound.
A program may use at most 64 MiB of HBM per device.

v0:
```python
import jax
import jax.numpy as jnp
from jax import lax
from jax.sharding import PartitionSpec as P


def slot_targets(ids, partner, experts, capacity):
    flat = ids.reshape(-1)
    onehot = (flat[:, None] == jnp.arange(experts, dtype=jnp.int32)[None, :]).astype(jnp.int32)
    ranks = jnp.sum((jnp.cumsum(onehot, axis=0) - 1) * onehot, axis=1)
    spare_of = jnp.sum(onehot * partner[None, :], axis=1)
    server = jnp.where(ranks >= capacity, spare_of, flat)
    return server * (2 * capacity) + ranks


def per_device(
    tokens,
    route_ids,
    route_weights,
    modulation,
    partner,
    w_gate,
    w_up,
    w_down,
    spare_gate,
    spare_up,
    spare_down,
):
    experts = lax.axis_size("expert")
    shards = lax.axis_size("tensor")
    rows, width = tokens.shape
    capacity = 2 * rows // experts
    columns = width // shards
    mod_row = modulation[0]
    tensor_start = lax.axis_index("tensor") * columns
    values = tokens.astype(jnp.float32)
    mean = jnp.mean(values, axis=1, keepdims=True)
    centred = values - mean
    var = jnp.mean(centred * centred, axis=1, keepdims=True)
    normed = centred / jnp.sqrt(var + 1e-06)
    modded = (normed * (1.0 + mod_row[width : 2 * width]) + mod_row[0:width]).astype(jnp.bfloat16)
    targets = slot_targets(route_ids, partner, experts, capacity)
    features = modded.shape[1]
    spread = jnp.repeat(modded, 2, axis=0)
    outgoing = jnp.zeros((experts * 2 * capacity, features), jnp.bfloat16).at[targets].set(spread)
    outgoing = outgoing.reshape(experts, 2, capacity, features)
    home_set = (w_gate[0], w_up[0], w_down[0])
    spare_set = (spare_gate[0], spare_up[0], spare_down[0])

    def project(block, weight_sets):
        count = block.shape[2]
        which = 0
        weight_set = weight_sets[which]
        flat_rows = block[:, which].reshape(experts * count, width)
        gate_sum = jnp.dot(flat_rows, weight_set[0], preferred_element_type=jnp.float32)
        up_sum = jnp.dot(flat_rows, weight_set[1], preferred_element_type=jnp.float32)
        products = [(gate_sum, up_sum)]
        which = 0
        gate_sum, up_sum = products[which]
        hidden = (jax.nn.silu(gate_sum) * up_sum).astype(jnp.bfloat16)
        rounded = jnp.dot(hidden, weight_sets[which][2], preferred_element_type=jnp.float32).astype(
            jnp.bfloat16
        )
        pieces = rounded.astype(jnp.float32).reshape(experts, 1, count, width)
        shares = lax.psum_scatter(
            pieces.astype(jnp.bfloat16), "tensor", scatter_dimension=3, tiled=True
        ).astype(jnp.float32)
        return lax.all_to_all(
            shares.astype(jnp.bfloat16), "expert", split_axis=0, concat_axis=0, tiled=True
        ).astype(shares.dtype)

    home_back = project(
        lax.all_to_all(outgoing[:, 0:1], "expert", split_axis=0, concat_axis=0, tiled=True),
        (home_set,),
    )
    spill_back = project(
        lax.all_to_all(outgoing[:, 1:2], "expert", split_axis=0, concat_axis=0, tiled=True),
        (spare_set,),
    )
    returned = jnp.concatenate((home_back, spill_back), axis=1)
    flat_back = returned.reshape(experts * 2 * capacity, columns)
    picked = flat_back[targets].reshape(rows, 2, columns)
    mixed = jnp.sum(picked * route_weights[:, :, None], axis=1)
    own_cols = lax.dynamic_slice_in_dim(values, tensor_start, columns, 1)
    gate_cols = lax.dynamic_slice_in_dim(mod_row, 2 * width + tensor_start, columns, 0)
    return (own_cols + gate_cols[None, :] * mixed).astype(jnp.bfloat16)


def solution(mesh):
    placed = (
        P(("groups", "expert"), None),
        P(("groups", "expert"), None),
        P(("groups", "expert"), None),
        P(("groups", "expert"), None),
        P(),
        P("expert", None, "tensor"),
        P("expert", None, "tensor"),
        P("expert", "tensor", None),
        P("expert", None, "tensor"),
        P("expert", None, "tensor"),
        P("expert", "tensor", None),
    )
    return jax.shard_map(
        per_device,
        mesh=mesh,
        in_specs=placed,
        out_specs=P(("groups", "expert"), "tensor"),
        check_vma=False,
    )
```

profile of v0, /device:TPU:0, one launch (start us, length us, event | category | flops | bytes accessed | tf_op | source)
XLA Modules:
  0.0 186.8 jit_solution(12211462042598215440)
XLA Ops:
  6.5 0.9 copy.19
  7.9 1.2 reduce-window.6
  10.3 1.4 convert_reduce_fusion
  12.7 1.3 broadcast_in_dim.5
  14.0 2.2 %reshape.141 = bf16[512,2048]{1,0:T(8,128)(2,1)} reshape(bf16[256,2,2048]{2,1,0:T(2,128)(2,1)S(1)} %broadcast_in_dim.5) | data formatting | bytes 4194304 | tf_op jit(solution)/shard_map/reshape | solution.py:44
  16.3 7.2 %scatter_custom_fusion = bf16[1024,2048]{1,0:T(8,128)(2,1)} fusion(s32[512]{0:T(512)S(1)} %bitcast.78, bf16[512,2048]{1,0:T(8,128)(2,1)} %reshape.141, bf16[]{:T(256)} %constant.14.clone.1), kind=kCustom, calls=%fused_computation.20 | custom fusion | bytes 4194816 | tf_op jit(solution)/shard_map/scatter | solution.py:45
  23.5 2.6 %fusion.35 = (bf16[4,1,128,2048]{3,2,1,0:T(8,128)(2,1)S(1)}, bf16[4,1,128,2048]{3,2,1,0:T(8,128)(2,1)S(1)}) fusion(bf16[4,2,128,2048]{3,2,1,0:T(8,128)(2,1)} %bitcast.67), kind=kLoop, calls=%fused_computation.47 | loop fusion | bytes 8388608 | tf_op jit(solution)/shard_map/slice | solution.py:73
  26.2 30.0 %all_to_all.20 = bf16[4,1,128,2048]{3,2,1,0:T(8,128)(2,1)S(1)} all-to-all(bf16[4,1,128,2048]{3,2,1,0:T(8,128)(2,1)S(1)} %get-tuple-element.7), channel_id=1, replica_groups=mesh['groups'=2,'expert'=4,'tensor'=4] {'expert'}, dimensions={0} | all-to-all | bytes 4194304 | tf_op jit(solution)/shard_map/all_to_all | solution.py:73
  56.2 1.3 copy-done.1
  57.5 3.6 %fusion.10 = f32[512,1024]{1,0:T(8,128)} fusion(bf16[512,2048]{1,0:T(8,128)(2,1)S(1)} %bitcast.70, bf16[1,2048,1024]{2,1,0:T(8,128)(2,1)S(1)} %copy-done.5), kind=kOutput, calls=%fused_computation.12 | convolution fusion | flops 2147483648 | bytes 8388608 | tf_op jit(solution)/shard_map/dot_general | solution.py:55
  61.1 10.6 %fusion.12 = bf16[512,2048]{1,0:T(8,128)(2,1)} fusion(bf16[1,1024,2048]{2,1,0:T(8,128)(2,1)} %param.18, f32[512,1024]{1,0:T(8,128)} %fusion.10, bf16[512,2048]{1,0:T(8,128)(2,1)} %bitcast.71, bf16[1,2048,1024]{2,1,0:T(8,128)(2,1)} %param.17), kind=kOutput, calls=%fused_computation.14 | convolution fusion | flops 4299161600 | bytes 14680064 | tf_op jit(solution)/shard_map/dot_general | solution.py:61
  71.8 28.4 %all_to_all.21 = bf16[4,1,128,2048]{3,2,1,0:T(8,128)(2,1)S(1)} all-to-all(bf16[4,1,128,2048]{3,2,1,0:T(8,128)(2,1)S(1)} %get-tuple-element.8), channel_id=1, replica_groups=mesh['groups'=2,'expert'=4,'tensor'=4] {'expert'}, dimensions={0} | all-to-all | bytes 4194304 | tf_op jit(solution)/shard_map/all_to_all | solution.py:77
  100.2 1.3 copy-done.2
  101.6 2.3 %fusion.4 = f32[512,1024]{1,0:T(8,128)S(1)} fusion(bf16[512,2048]{1,0:T(8,128)(2,1)S(1)} %bitcast.72, bf16[1,2048,1024]{2,1,0:T(8,128)(2,1)S(1)} %copy-done.6), kind=kOutput, calls=%fused_computation.6 | convolution fusion | flops 2147483648 | bytes 8388608 | tf_op jit(solution)/shard_map/dot_general | solution.py:55
  103.9 10.0 %fusion.15 = bf16[512,2048]{1,0:T(8,128)(2,1)} fusion(bf16[1,1024,2048]{2,1,0:T(8,128)(2,1)} %param.21, f32[512,1024]{1,0:T(8,128)S(1)} %fusion.4, bf16[512,2048]{1,0:T(8,128)(2,1)} %bitcast.73, bf16[1,2048,1024]{2,1,0:T(8,128)(2,1)} %param.20), kind=kOutput, calls=%fused_computation.15 | convolution fusion | flops 4299161600 | bytes 14680064 | tf_op jit(solution)/shard_map/dot_general | solution.py:61
  113.9 2.2 %reduce-scatter.3.cloned.1.call-done = bf16[4,1,128,512]{3,2,1,0:T(8,128)(2,1)} async-done(((bf16[4,1,128,2048]{3,2,1,0:T(8,128)(2,1)}), bf16[4,1,128,512]{3,2,1,0:T(8,128)(2,1)}) %reduce-scatter.3.cloned.1.call-update) | async-done | bytes 524304 | tf_op jit(solution)/shard_map/reduce_scatter | solution.py:65
  116.1 3.5 %all-to-all-start.1 = ((bf16[4,1,128,512]{3,2,1,0:T(8,128)(2,1)}), bf16[4,1,128,512]{3,2,1,0:T(8,128)(2,1)S(1)}, u32[]{:S(2)}, u32[]{:S(2)}) async-start(bf16[4,1,128,512]{3,2,1,0:T(8,128)(2,1)} %reduce-scatter.3.cloned.1.call-done), calls=%async_computation.2 | async-start | bytes 1048576 | tf_op jit(solution)/shard_map/all_to_all | solution.py:68
  119.6 42.1 %reduce-scatter.5.cloned.1.call-done = bf16[4,1,128,512]{3,2,1,0:T(8,128)(2,1)} async-done(((bf16[4,1,128,2048]{3,2,1,0:T(8,128)(2,1)}), bf16[4,1,128,512]{3,2,1,0:T(8,128)(2,1)}) %reduce-scatter.5.cloned.1.call-update) | async-done | bytes 524304 | tf_op jit(solution)/shard_map/reduce_scatter | solution.py:65
  161.7 3.7 %all-to-all-start.3 = ((bf16[4,1,128,512]{3,2,1,0:T(8,128)(2,1)}), bf16[4,1,128,512]{3,2,1,0:T(8,128)(2,1)S(1)}, u32[]{:S(2)}, u32[]{:S(2)}) async-start(bf16[4,1,128,512]{3,2,1,0:T(8,128)(2,1)} %reduce-scatter.5.cloned.1.call-done), calls=%async_computation.5 | async-start | bytes 1048576 | tf_op jit(solution)/shard_map/all_to_all | solution.py:68
  165.4 1.6 convert_element_type.58
  167.9 6.1 %all-to-all-done.3 = bf16[4,1,128,512]{3,2,1,0:T(8,128)(2,1)S(1)} async-done(((bf16[4,1,128,512]{3,2,1,0:T(8,128)(2,1)}), bf16[4,1,128,512]{3,2,1,0:T(8,128)(2,1)S(1)}, u32[]{:S(2)}, u32[]{:S(2)}) %all-to-all-start.3) | async-done | bytes 524320 | tf_op jit(solution)/shard_map/all_to_all | solution.py:68
  174.5 1.6 gather_fusion
  176.7 1.3 multiply_reduce_fusion.1
  178.1 1.9 add_convert_fusion.1
  (37 shorter events, 4.6 us)
Async XLA Ops:
  6.5 5.2 %copy-start = (bf16[256,2048]{1,0:T(8,128)(2,1)S(1)}, bf16[256,2048]{1,0:T(8,128)(2,1)}, u32[]{:S(2)}) copy-start(bf16[256,2048]{1,0:T(8,128)(2,1)} %param.11) | copy-start | bytes 3145732
  6.5 109.6 %reduce-scatter.3.cloned.1.call-start = ((), (), s32[]{:S(2)}) async-start(), calls=%async_computation.6 | async-start | bytes 2621440 | tf_op jit(solution)/shard_map/reduce_scatter | solution.py:65
  14.0 2.3 %copy-start.4 = (s32[4]{0:T(128)S(1)}, s32[4]{0:T(128)}, u32[]{:S(2)}) copy-start(s32[4]{0:T(128)} %param.15) | copy-start | bytes 52
  26.2 31.3 %copy-start.5 = (bf16[1,2048,1024]{2,1,0:T(8,128)(2,1)S(1)}, bf16[1,2048,1024]{2,1,0:T(8,128)(2,1)}, u32[]{:S(2)}) copy-start(bf16[1,2048,1024]{2,1,0:T(8,128)(2,1)} %param.16) | copy-start | bytes 12582916
  56.2 1.3 copy-start.1
  71.7 90.0 %reduce-scatter.5.cloned.1.call-start = ((), (), s32[]{:S(2)}) async-start(), calls=%async_computation.7 | async-start | bytes 2621440 | tf_op jit(solution)/shard_map/reduce_scatter | solution.py:65
  71.8 29.8 %copy-start.6 = (bf16[1,2048,1024]{2,1,0:T(8,128)(2,1)S(1)}, bf16[1,2048,1024]{2,1,0:T(8,128)(2,1)}, u32[]{:S(2)}) copy-start(bf16[1,2048,1024]{2,1,0:T(8,128)(2,1)} %param.19) | copy-start | bytes 12582916
  100.2 1.3 copy-start.2
  116.1 45.6 %all-to-all-start.1 = ((bf16[4,1,128,512]{3,2,1,0:T(8,128)(2,1)}), bf16[4,1,128,512]{3,2,1,0:T(8,128)(2,1)S(1)}, u32[]{:S(2)}, u32[]{:S(2)}) async-start(bf16[4,1,128,512]{3,2,1,0:T(8,128)(2,1)} %reduce-scatter.3.cloned.1.call-done), calls=%async_computation.2 | async-start | bytes 1048576 | tf_op jit(solution)/shard_map/all_to_all | solution.py:68
  119.6 47.5 %copy-start.3 = (f32[256,2]{0,1:T(2,128)S(1)}, f32[256,2]{0,1:T(2,128)}, u32[]{:S(2)}) copy-start(f32[256,2]{0,1:T(2,128)} %param.13) | copy-start | bytes 6148
  161.7 12.3 %all-to-all-start.3 = ((bf16[4,1,128,512]{3,2,1,0:T(8,128)(2,1)}), bf16[4,1,128,512]{3,2,1,0:T(8,128)(2,1)S(1)}, u32[]{:S(2)}, u32[]{:S(2)}) async-start(bf16[4,1,128,512]{3,2,1,0:T(8,128)(2,1)} %reduce-scatter.5.cloned.1.call-done), calls=%async_computation.5 | async-start | bytes 1048576 | tf_op jit(solution)/shard_map/all_to_all | solution.py:68
Sparse Core Ops, SparseCore 0:
  71.9 44.1 reduce-scatter.2
  118.5 43.1 reduce-scatter.4
where the time goes:
time: 187 us
  blocking collectives  58.4 us (31%)
  waiting for transfers between devices  50.5 us (27%)
  matrix products  26.5 us (14%)
  local copies, waits for them, and re-layouts  20.6 us (11%)
  between operations  13.6 us (7%)
  other arithmetic  9.89 us (5%)
  starting transfers between devices  7.2 us (4%)
    reduce_scatter x2, waiting for transfers between devices, project(): lax.psum_scatter(pieces.astype(jnp.bfloat16), 'tensor', scatter_dimension...  44.3 us
    all_to_all x1, blocking collectives, per_device(): lax.all_to_all(outgoing[:, 0:1], 'expert', split_axis=0, concat_axis=0, t...  30 us
    all_to_all x1, blocking collectives, per_device(): lax.all_to_all(outgoing[:, 1:2], 'expert', split_axis=0, concat_axis=0, t...  28.4 us
    dot_general x2, matrix products, project(): jnp.dot(hidden, weight_sets[which][2], preferred_element_type=jnp.float32)  20.5 us
    scatter x1, local copies, waits for them, and re-layouts, per_device(): jnp.zeros((experts * 2 * capacity, features), jnp.bfloat16).at[targets]  7.21 us
    all_to_all x2, starting transfers between devices, project(): lax.all_to_all(shares.astype(jnp.bfloat16), 'expert', split_axis=0, conca...  7.16 us
    all_to_all x2, waiting for transfers between devices, project(): lax.all_to_all(shares.astype(jnp.bfloat16), 'expert', split_axis=0, conca...  6.15 us
    dot_general x2, matrix products, project(): jnp.dot(flat_rows, weight_set[0], preferred_element_type=jnp.float32)  5.99 us
  transfers between devices with their start and end apart: 4, of which 3 were waited for; matrix products, arithmetic and copies ran while one was open for 8% of the time, Pallas kernels for 0%

commit v1 on v0

v1 whole, which is shorter than its diff:
```python
import jax
import jax.numpy as jnp
from jax import lax
from jax.sharding import PartitionSpec as P


CHUNKS = 2


def dot32(a, b):
    return jnp.dot(a, b, preferred_element_type=jnp.float32)


def pair_targets(ids, partner, experts, capacity):
    rows = ids.shape[0]
    onehot = (ids[:, :, None] == jnp.arange(experts, dtype=jnp.int32)).astype(jnp.float32)
    named = (onehot[:, 0] + onehot[:, 1]).astype(jnp.bfloat16)
    order = jnp.arange(rows, dtype=jnp.int32)
    before = (order[:, None] > order[None, :]).astype(jnp.bfloat16)
    earlier = dot32(before, named)
    ranks = jnp.sum(onehot * earlier[:, None, :], axis=2).astype(jnp.int32)
    spare_of = jnp.sum(onehot * partner.astype(jnp.float32), axis=2).astype(jnp.int32)
    server = jnp.where(ranks >= capacity, spare_of, ids)
    return server * (2 * capacity) + ranks


def modulate(values, mod_row, width):
    mean = jnp.mean(values, axis=1, keepdims=True)
    centred = values - mean
    var = jnp.mean(centred * centred, axis=1, keepdims=True)
    normed = centred / jnp.sqrt(var + 1e-06)
    return (normed * (1.0 + mod_row[width : 2 * width]) + mod_row[0:width]).astype(jnp.bfloat16)


def hidden_of(rows, gate, up):
    return (jax.nn.silu(dot32(rows, gate)) * dot32(rows, up)).astype(jnp.bfloat16)


def by_tokens(modded, targets, weights, capacity, experts, shards, sets):
    rows, width = modded.shape
    columns = width // shards
    slots = 2 * capacity
    me = lax.axis_index("expert")
    packed = jnp.concatenate((targets.astype(jnp.float32), weights), axis=1).T
    routes = lax.all_gather(packed, "expert")
    seen = lax.all_gather(modded, "expert")
    local = routes[:, 0:2].astype(jnp.int32) - me * slots
    number = jnp.arange(slots, dtype=jnp.int32)[None, :, None]
    hits = [local[:, j][:, None, :] == number for j in range(2)]
    pick = (hits[0] | hits[1]).astype(jnp.bfloat16)
    factor = sum(
        jnp.sum(jnp.where(hits[j], routes[:, 2 + j][:, None, :], 0.0), axis=2) for j in range(2)
    )
    hidden = []
    for which, (gate, up, _) in enumerate(sets):
        part = slice(which * capacity, (which + 1) * capacity)
        arrived = lax.dot_general(
            pick[:, part], seen, (((2,), (1,)), ((0,), (0,))), preferred_element_type=jnp.float32
        ).astype(jnp.bfloat16)
        hidden.append(hidden_of(arrived.reshape(experts * capacity, width), gate, up))
    sums = []
    step = columns // CHUNKS
    for c in range(CHUNKS):
        done = []
        for which, (_, _, down) in enumerate(sets):
            piece = down.reshape(-1, shards, columns)[:, :, c * step : (c + 1) * step]
            out = dot32(hidden[which], piece.reshape(-1, shards * step))
            out = out.reshape(experts, capacity, shards * step)
            scale = factor[:, which * capacity : (which + 1) * capacity]
            done.append((out * scale[:, :, None]).astype(jnp.bfloat16))
        served = jnp.concatenate(done, axis=1)
        part = lax.dot_general(
            pick, served, (((1,), (1,)), ((0,), (0,))), preferred_element_type=jnp.float32
        ).astype(jnp.bfloat16)
        own = lax.psum_scatter(
            part.reshape(experts * rows, shards * step), "expert", scatter_dimension=0, tiled=True
        )
        sums.append(lax.psum_scatter(own, "tensor", scatter_dimension=1, tiled=True))
    return jnp.concatenate(sums, axis=1).astype(jnp.float32)


def by_slots(modded, targets, weights, capacity, experts, shards, sets):
    rows, width = modded.shape
    columns = width // shards
    slots = experts * 2 * capacity
    number = jnp.arange(slots, dtype=jnp.int32)
    hits = [targets[:, j][:, None] == number[None, :] for j in range(2)]
    pick = (hits[0] | hits[1]).astype(jnp.bfloat16)
    outgoing = lax.dot_general(
        pick, modded, (((0,), (0,)), ((), ())), preferred_element_type=jnp.float32
    ).astype(jnp.bfloat16)
    outgoing = outgoing.reshape(experts, 2, capacity, width)
    back = []
    for which, (gate, up, down) in enumerate(sets):
        arrived = lax.all_to_all(
            outgoing[:, which], "expert", split_axis=0, concat_axis=0, tiled=True
        ).reshape(experts * capacity, width)
        part = dot32(hidden_of(arrived, gate, up), down).astype(jnp.bfloat16)
        shares = lax.psum_scatter(part, "tensor", scatter_dimension=1, tiled=True)
        back.append(
            lax.all_to_all(
                shares.reshape(experts, capacity, columns),
                "expert",
                split_axis=0,
                concat_axis=0,
                tiled=True,
            )
        )
    flat = jnp.stack(back, axis=1).reshape(slots, columns)
    return sum(
        dot32(hits[j].astype(jnp.bfloat16), flat) * weights[:, j : j + 1] for j in range(2)
    )


def per_device(
    tokens,
    route_ids,
    route_weights,
    modulation,
    partner,
    w_gate,
    w_up,
    w_down,
    spare_gate,
    spare_up,
    spare_down,
):
    experts = lax.axis_size("expert")
    shards = lax.axis_size("tensor")
    rows, width = tokens.shape
    capacity = 2 * rows // experts
    columns = width // shards
    mod_row = modulation[0]
    tensor_start = lax.axis_index("tensor") * columns
    modded = modulate(tokens.astype(jnp.float32), mod_row, width)
    targets = pair_targets(route_ids, partner, experts, capacity)
    sets = ((w_gate[0], w_up[0], w_down[0]), (spare_gate[0], spare_up[0], spare_down[0]))
    plan = by_tokens if 2 * capacity >= rows else by_slots
    mixed = plan(modded, targets, route_weights, capacity, experts, shards, sets)
    own_cols = lax.dynamic_slice_in_dim(tokens, tensor_start, columns, 1).astype(jnp.float32)
    gate_cols = lax.dynamic_slice_in_dim(mod_row, 2 * width + tensor_start, columns, 0)
    return (own_cols + gate_cols[None, :] * mixed).astype(jnp.bfloat16)


def solution(mesh):
    placed = (
        P(("groups", "expert"), None),
        P(("groups", "expert"), None),
        P(("groups", "expert"), None),
        P(("groups", "expert"), None),
        P(),
        P("expert", None, "tensor"),
        P("expert", None, "tensor"),
        P("expert", "tensor", None),
        P("expert", None, "tensor"),
        P("expert", None, "tensor"),
        P("expert", "tensor", None),
    )
    return jax.shard_map(
        per_device,
        mesh=mesh,
        in_specs=placed,
        out_specs=P(("groups", "expert"), "tensor"),
        check_vma=False,
    )
```

time: 187 us -> 196 us (1.048)
  blocking collectives: 58.4 us -> 6.38 us
  waiting for transfers between devices: 50.5 us -> 100 us
  local copies, waits for them, and re-layouts: 20.6 us -> 42 us
  starting transfers between devices: 7.2 us -> 0.17 us
  other arithmetic: 9.89 us -> 7.18 us
    all_to_all x2 -> x0, blocking collectives: 58.4 us -> none  [the longest x1 30 us: per_device(): lax.all_to_all(outgoing[:, 0:1], 'expert', split_axis=0, concat_axis=0, t...]
    reduce_scatter x2 -> x4, waiting for transfers between devices: 44.3 us -> 99.9 us  [the longest x2 54.1 us: by_tokens(): lax.psum_scatter(part.reshape(experts * rows, shards * step), 'expert', s...]
    another operation x0 -> x2, local copies, waits for them, and re-layouts: none -> 15.8 us  [by_tokens(): piece = down.reshape(-1, shards, columns)[:, :, c * step:(c + 1) * step]]
    reshape x3 -> x4, local copies, waits for them, and re-layouts: 3.01 us -> 14.9 us  [by_tokens(): out = dot32(hidden[which], piece.reshape(-1, shards * step))]
    scatter x1 -> x0, local copies, waits for them, and re-layouts: 7.21 us -> none  [per_device(): jnp.zeros((experts * 2 * capacity, features), jnp.bfloat16).at[targets]]
    all_to_all x2 -> x0, starting transfers between devices: 7.16 us -> none  [project(): lax.all_to_all(shares.astype(jnp.bfloat16), 'expert', split_axis=0, conca...]
    all_gather x0 -> x1, blocking collectives: none -> 6.38 us  [by_tokens(): routes = lax.all_gather(packed, 'expert')]
    all_to_all x2 -> x0, waiting for transfers between devices: 6.15 us -> none  [project(): lax.all_to_all(shares.astype(jnp.bfloat16), 'expert', split_axis=0, conca...]
  transfers between devices with their start and end apart: 4 -> 5, of which waited for: 3 -> 4; matrix products, arithmetic and copies ran while one was open for 8% -> 24% of each run, Pallas kernels for 0% -> 0%
where the time goes in v1:
time: 196 us; the launch traced here: 195 us
  waiting for transfers between devices  100 us (51%)
  local copies, waits for them, and re-layouts  42 us (21%)
  matrix products  25.6 us (13%)
  between operations  13.5 us (7%)
  other arithmetic  7.18 us (4%)
  blocking collectives  6.38 us (3%)
    reduce_scatter x2, waiting for transfers between devices, by_tokens(): lax.psum_scatter(part.reshape(experts * rows, shards * step), 'expert', s...  54.1 us
    reduce_scatter x2, waiting for transfers between devices, by_tokens(): lax.psum_scatter(own, 'tensor', scatter_dimension=1, tiled=True)  45.8 us
    dot_general x9, matrix products, dot32(): return jnp.dot(a, b, preferred_element_type=jnp.float32)  17.3 us
    another operation x2, local copies, waits for them, and re-layouts, by_tokens(): piece = down.reshape(-1, shards, columns)[:, :, c * step:(c + 1) * step]  15.8 us
    reshape x4, local copies, waits for them, and re-layouts, by_tokens(): out = dot32(hidden[which], piece.reshape(-1, shards * step))  14.9 us
    slice x2, local copies, waits for them, and re-layouts, by_tokens(): piece = down.reshape(-1, shards, columns)[:, :, c * step:(c + 1) * step]  8.6 us
    all_gather x1, blocking collectives, by_tokens(): routes = lax.all_gather(packed, 'expert')  6.38 us
    dot_general x2, matrix products, by_tokens(): lax.dot_general(pick, served, (((1,), (1,)), ((0,), (0,))), preferred_ele...  4.54 us
  transfers between devices with their start and end apart: 5, of which 4 were waited for; matrix products, arithmetic and copies ran while one was open for 24% of the time, Pallas kernels for 0%

profile of v1, /device:TPU:0, one launch (start us, length us, event | category | flops | bytes accessed | tf_op | source)
XLA Modules:
  0.0 194.9 jit_solution(11449930385608822941)
XLA Ops:
  6.5 1.5 convert_reduce_fusion
  8.1 1.6 fusion.10
  11.3 7.9 %reshape_squeeze.8 = bf16[1024,4,512]{2,1,0:T(4,128)(2,1)} reshape(bf16[1,1024,2048]{2,1,0:T(8,128)(2,1)} %param.18) | data formatting | bytes 8388608 | tf_op jit(solution)/shard_map/reshape;squeeze | solution.py:66
  19.2 4.2 %fusion.48 = (bf16[1024,4,256]{2,1,0:T(4,128)(2,1)}, bf16[1024,4,256]{2,1,0:T(4,128)(2,1)S(1)}) fusion(bf16[1024,4,512]{2,1,0:T(4,128)(2,1)} %reshape_squeeze.8), kind=kLoop, calls=%fused_computation.68 | loop fusion | bytes 8388608 | tf_op jit(solution)/shard_map/slice | solution.py:66
  23.5 4.5 %reshape.69 = bf16[1024,1024,1]{1,0,2:T(8,128)(2,1)} reshape(bf16[1024,4,256]{2,1,0:T(4,128)(2,1)} %get-tuple-element.7) | data formatting | bytes 4194304 | tf_op jit(solution)/shard_map/reshape | solution.py:67
  28.0 7.9 %reshape_squeeze.9 = bf16[1024,4,512]{2,1,0:T(4,128)(2,1)} reshape(bf16[1,1024,2048]{2,1,0:T(8,128)(2,1)} %param.21) | data formatting | bytes 8388608 | tf_op jit(solution)/shard_map/reshape;squeeze | solution.py:66
  35.9 4.4 %fusion.49 = (bf16[1024,4,256]{2,1,0:T(4,128)(2,1)}, bf16[1024,4,256]{2,1,0:T(4,128)(2,1)}) fusion(bf16[1024,4,512]{2,1,0:T(4,128)(2,1)} %reshape_squeeze.9), kind=kLoop, calls=%fused_computation.69 | loop fusion | bytes 8388608 | tf_op jit(solution)/shard_map/slice | solution.py:66
  40.3 4.5 %reshape.70 = bf16[1024,1024,1]{1,0,2:T(8,128)(2,1)} reshape(bf16[1024,4,256]{2,1,0:T(4,128)(2,1)} %get-tuple-element.9) | data formatting | bytes 4194304 | tf_op jit(solution)/shard_map/reshape | solution.py:67
  45.0 6.4 %all-gather.2 = f32[4,4,256]{2,1,0:T(4,128)S(1)} all-gather(f32[1,4,256]{2,1,0:T(4,128)S(1)} %maximum_bitcast_fusion), channel_id=2, replica_groups=mesh['groups'=2,'expert'=4,'tensor'=4] {'expert'}, dimensions={0}, use_global_device_ids=true | all-gather | bytes 20480 | tf_op jit(solution)/shard_map/all_gather | solution.py:45
  52.2 3.1 %convolution_convert_fusion = bf16[4,128,2048]{2,1,0:T(8,128)(2,1)S(1)} fusion(bf16[4,256,2048]{2,1,0:T(8,128)(2,1)} %bitcast.55, pred[4,256,256]{2,1,0:T(32,128)(4,1)S(1)} %fusion.32), kind=kOutput, calls=%fused_computation.8 | convolution fusion | flops 537919488 | bytes 6422528 | tf_op jit(solution)/shard_map/dot_general | solution.py:57
  57.8 2.3 %fusion.2 = f32[512,1024]{1,0:T(8,128)S(1)} fusion(bf16[512,2048]{1,0:T(8,128)(2,1)S(1)} %bitcast.59, bf16[1,2048,1024]{2,1,0:T(8,128)(2,1)S(1)} %copy-done.7), kind=kOutput, calls=%fused_computation.2 | convolution fusion | flops 2147483648 | bytes 8388608 | tf_op jit(solution)/shard_map/dot_general | solution.py:11
  60.2 2.5 %multiply_convert_fusion.3 = bf16[512,1024]{1,0:T(8,128)(2,1)S(1)} fusion(f32[512,1024]{1,0:T(8,128)S(1)} %fusion.2, bf16[512,2048]{1,0:T(8,128)(2,1)S(1)} %bitcast.60, bf16[1,2048,1024]{2,1,0:T(8,128)(2,1)S(1)} %copy-done.8), kind=kOutput, calls=%fused_computation.29 | convolution fusion | flops 2150629376 | bytes 9437184 | tf_op jit(solution)/shard_map/dot_general | solution.py:11
  62.7 2.3 %fusion.6 = f32[512,1024]{1,0:T(8,128)S(1)} fusion(bf16[512,2048]{1,0:T(8,128)(2,1)S(1)} %bitcast.57, bf16[1,2048,1024]{2,1,0:T(8,128)(2,1)S(1)} %copy-done.9), kind=kOutput, calls=%fused_computation.6 | convolution fusion | flops 2147483648 | bytes 8388608 | tf_op jit(solution)/shard_map/dot_general | solution.py:11
  65.3 2.5 %multiply_convert_fusion.5 = bf16[512,1024]{1,0:T(8,128)(2,1)S(1)} fusion(f32[512,1024]{1,0:T(8,128)S(1)} %fusion.6, bf16[512,2048]{1,0:T(8,128)(2,1)S(1)} %bitcast.58, bf16[1,2048,1024]{2,1,0:T(8,128)(2,1)S(1)} %copy-done.10), kind=kOutput, calls=%fused_computation.31 | convolution fusion | flops 2150629376 | bytes 9437184 | tf_op jit(solution)/shard_map/dot_general | solution.py:11
  71.1 2.4 %fusion.25 = bf16[4,256,1024]{2,1,0:T(8,128)(2,1)} fusion(bf16[4,128,1024]{2,1,0:T(8,128)(2,1)S(1)} %multiply_convert_fusion.2, bf16[4,128,1024]{2,1,0:T(8,128)(2,1)S(1)} %multiply_convert_fusion.4, s32[4,256]{1,0:T(4,128)S(1)} %get-tuple-element.21, s32[4,256]{1,0:T(4,128)S(1)} %get-tuple-element.22), kind=kOutput, calls=%fused_computation.33 | convolution fusion | flops 542900224 | bytes 4202496 | tf_op jit(solution)/shard_map/dot_general | solution.py:72
  73.5 2.7 %reshape.71 = bf16[1024,1024,1]{1,0,2:T(8,128)(2,1)} reshape(bf16[1024,4,256]{2,1,0:T(4,128)(2,1)S(1)} %get-tuple-element.8) | data formatting | bytes 4194304 | tf_op jit(solution)/shard_map/reshape | solution.py:67
  76.3 3.2 %reshape.72 = bf16[1024,1024,1]{1,0,2:T(8,128)(2,1)S(1)} reshape(bf16[1024,4,256]{2,1,0:T(4,128)(2,1)} %get-tuple-element.10) | data formatting | bytes 4194304 | tf_op jit(solution)/shard_map/reshape | solution.py:67
  79.5 3.6 %multiply_convert_fusion.1 = bf16[4,128,1024]{2,1,0:T(8,128)(2,1)S(1)} fusion(bf16[4,128,1024]{2,1,0:T(8,128)(2,1)} %bitcast.69, bf16[1024,1024,1]{1,0,2:T(8,128)(2,1)} %reshape.71, f32[4,128]{1,0:T(4,128)S(1)} %get-tuple-element.17), kind=kOutput, calls=%fused_computation.27 | convolution fusion | flops 1074790400 | bytes 4196352 | tf_op jit(solution)/shard_map/dot_general | solution.py:11
  84.4 2.1 %fusion.22 = bf16[4,256,1024]{2,1,0:T(8,128)(2,1)} fusion(bf16[4,128,1024]{2,1,0:T(8,128)(2,1)S(1)} %multiply_convert_fusion, bf16[4,128,1024]{2,1,0:T(8,128)(2,1)S(1)} %multiply_convert_fusion.1, s32[4,256]{1,0:T(4,128)S(1)} %get-tuple-element.21, s32[4,256]{1,0:T(4,128)S(1)} %get-tuple-element.22), kind=kOutput, calls=%fused_computation.32 | convolution fusion | flops 542900224 | bytes 4202496 | tf_op jit(solution)/shard_map/dot_general | solution.py:72
  86.6 20.0 %reduce-scatter.5.cloned.1.call-done = bf16[256,1024]{1,0:T(8,128)(2,1)} async-done(((bf16[1024,1024]{1,0:T(8,128)(2,1)}), bf16[256,1024]{1,0:T(8,128)(2,1)}) %reduce-scatter.5.cloned.1.call-update) | async-done | bytes 524304 | tf_op jit(solution)/shard_map/reduce_scatter | solution.py:75
  106.7 34.1 %reduce-scatter.9.cloned.1.call-done = bf16[256,1024]{1,0:T(8,128)(2,1)} async-done(((bf16[1024,1024]{1,0:T(8,128)(2,1)}), bf16[256,1024]{1,0:T(8,128)(2,1)}) %reduce-scatter.9.cloned.1.call-update) | async-done | bytes 524304 | tf_op jit(solution)/shard_map/reduce_scatter | solution.py:75
  140.8 23.8 %reduce-scatter.7.cloned.1.call-done = bf16[256,256]{1,0:T(8,128)(2,1)} async-done(((bf16[256,1024]{1,0:T(8,128)(2,1)}), bf16[256,256]{1,0:T(8,128)(2,1)}) %reduce-scatter.7.cloned.1.call-update) | async-done | bytes 131088 | tf_op jit(solution)/shard_map/reduce_scatter | solution.py:78
  164.6 22.0 %reduce-scatter.11.cloned.1.call-done = bf16[256,256]{1,0:T(8,128)(2,1)} async-done(((bf16[256,1024]{1,0:T(8,128)(2,1)}), bf16[256,256]{1,0:T(8,128)(2,1)}) %reduce-scatter.11.cloned.1.call-update) | async-done | bytes 131088 | tf_op jit(solution)/shard_map/reduce_scatter | solution.py:78
  186.6 1.7 add_convert_fusion
  (66 shorter events, 9.9 us)
Async XLA Ops:
  6.5 3.3 %copy-start.1 = (bf16[256,2048]{1,0:T(8,128)(2,1)S(1)}, bf16[256,2048]{1,0:T(8,128)(2,1)}, u32[]{:S(2)}) copy-start(bf16[256,2048]{1,0:T(8,128)(2,1)} %param.11) | copy-start | bytes 3145732
  6.5 3.2 %copy-start.5 = (f32[1,6144]{1,0:T(1,128)S(1)}, f32[1,6144]{1,0:T(1,128)}, u32[]{:S(2)}) copy-start(f32[1,6144]{1,0:T(1,128)} %param.14) | copy-start | bytes 73732
  6.5 45.6 %all-gather.5.cloned.1.call-start = ((), (), s32[]{:S(2)}) async-start(), calls=%async_computation.8 | async-start | bytes 5242880 | tf_op jit(solution)/shard_map/all_gather | solution.py:46
  8.1 3.2 %copy-start.11 = (s32[4]{0:T(128)S(1)}, s32[4]{0:T(128)}, u32[]{:S(2)}) copy-start(s32[4]{0:T(128)} %param.15) | copy-start | bytes 52
  11.3 95.3 %reduce-scatter.5.cloned.1.call-start = ((), (), s32[]{:S(2)}) async-start(), calls=%async_computation.4 | async-start | bytes 2621440 | tf_op jit(solution)/shard_map/reduce_scatter | solution.py:75
  40.3 4.5 %copy-start.4 = (s32[256,2]{0,1:T(2,128)S(1)}, s32[256,2]{0,1:T(2,128)}, u32[]{:S(2)}) copy-start(s32[256,2]{0,1:T(2,128)} %param.12) | copy-start | bytes 6148
  40.3 4.8 %copy-start.6 = (f32[256,2]{0,1:T(2,128)S(1)}, f32[256,2]{0,1:T(2,128)}, u32[]{:S(2)}) copy-start(f32[256,2]{0,1:T(2,128)} %param.13) | copy-start | bytes 6148
  52.2 3.5 %copy-start = (bf16[1024,2048]{1,0:T(8,128)(2,1)S(1)}, bf16[1024,2048]{1,0:T(8,128)(2,1)}, u32[]{:S(2)}) copy-start(bf16[1024,2048]{1,0:T(8,128)(2,1)} %all-gather.5.cloned.1.call-done) | copy-start | bytes 12582916
  55.6 2.2 %copy-start.7 = (bf16[1,2048,1024]{2,1,0:T(8,128)(2,1)S(1)}, bf16[1,2048,1024]{2,1,0:T(8,128)(2,1)}, u32[]{:S(2)}) copy-start(bf16[1,2048,1024]{2,1,0:T(8,128)(2,1)} %param.19) | copy-start | bytes 12582916
  57.8 2.4 %copy-start.8 = (bf16[1,2048,1024]{2,1,0:T(8,128)(2,1)S(1)}, bf16[1,2048,1024]{2,1,0:T(8,128)(2,1)}, u32[]{:S(2)}) copy-start(bf16[1,2048,1024]{2,1,0:T(8,128)(2,1)} %param.20) | copy-start | bytes 12582916
  60.2 2.6 %copy-start.9 = (bf16[1,2048,1024]{2,1,0:T(8,128)(2,1)S(1)}, bf16[1,2048,1024]{2,1,0:T(8,128)(2,1)}, u32[]{:S(2)}) copy-start(bf16[1,2048,1024]{2,1,0:T(8,128)(2,1)} %param.16) | copy-start | bytes 12582916
  62.7 6.4 %copy-start.12 = (bf16[512,1024]{1,0:T(8,128)(2,1)}, bf16[512,1024]{1,0:T(8,128)(2,1)S(1)}, u32[]{:S(2)}) copy-start(bf16[512,1024]{1,0:T(8,128)(2,1)S(1)} %multiply_convert_fusion.3) | copy-start | bytes 3145732
  62.7 2.6 %copy-start.10 = (bf16[1,2048,1024]{2,1,0:T(8,128)(2,1)S(1)}, bf16[1,2048,1024]{2,1,0:T(8,128)(2,1)}, u32[]{:S(2)}) copy-start(bf16[1,2048,1024]{2,1,0:T(8,128)(2,1)} %param.17) | copy-start | bytes 12582916
  65.3 2.5 %copy-start.2 = (bf16[1024,1024,1]{1,0,2:T(8,128)(2,1)S(1)}, bf16[1024,1024,1]{1,0,2:T(8,128)(2,1)}, u32[]{:S(2)}) copy-start(bf16[1024,1024,1]{1,0,2:T(8,128)(2,1)} %reshape.69) | copy-start | bytes 6291460
  67.8 1.3 copy-start.14
  67.8 2.0 %copy-start.3 = (bf16[1024,1024,1]{1,0,2:T(8,128)(2,1)S(1)}, bf16[1024,1024,1]{1,0,2:T(8,128)(2,1)}, u32[]{:S(2)}) copy-start(bf16[1024,1024,1]{1,0,2:T(8,128)(2,1)} %reshape.70) | copy-start | bytes 6291460
  73.5 67.3 %reduce-scatter.9.cloned.1.call-start = ((), (), s32[]{:S(2)}) async-start(), calls=%async_computation.6 | async-start | bytes 2621440 | tf_op jit(solution)/shard_map/reduce_scatter | solution.py:75
  79.5 3.6 %copy-start.13 = (bf16[512,1024]{1,0:T(8,128)(2,1)S(1)}, bf16[512,1024]{1,0:T(8,128)(2,1)}, u32[]{:S(2)}) copy-start(bf16[512,1024]{1,0:T(8,128)(2,1)} %copy-done.12) | copy-start | bytes 3145732
  86.5 78.1 %reduce-scatter.7.cloned.1.call-start = ((), (), s32[]{:S(2)}) async-start(), calls=%async_computation.5 | async-start | bytes 655360 | tf_op jit(solution)/shard_map/reduce_scatter | solution.py:78
  106.6 80.0 %reduce-scatter.11.cloned.1.call-start = ((), (), s32[]{:S(2)}) async-start(), calls=%async_computation.7 | async-start | bytes 655360 | tf_op jit(solution)/shard_map/reduce_scatter | solution.py:78
Sparse Core Ops, SparseCore 0:
  11.4 37.1 all-gather.4
  73.6 32.9 reduce-scatter.4
  109.3 31.4 reduce-scatter.8
  142.9 21.6 reduce-scatter.6
  166.7 19.8 reduce-scatter.10

commit v2 on v1

--- a/solution.py
+++ b/solution.py
@@ -36,47 +36,78 @@
     return (jax.nn.silu(dot32(rows, gate)) * dot32(rows, up)).astype(jnp.bfloat16)
 
 
+def swap(value, axis, bit):
+    count = lax.axis_size(axis)
+    return lax.ppermute(value, axis, [(i, i ^ bit) for i in range(count)])
+
+
+def gather_near(value, axis):
+    blocks = {0: value}
+    bit = lax.axis_size(axis) // 2
+    while bit:
+        blocks.update({r ^ bit: swap(v, axis, bit) for r, v in list(blocks.items())})
+        bit //= 2
+    return blocks
+
+
+def reduce_near(blocks, axis):
+    bit, count = 1, lax.axis_size(axis)
+    while bit < count:
+        sent = {r: swap(v.astype(jnp.bfloat16), axis, bit) for r, v in blocks.items() if r & bit}
+        blocks = {r: v + sent[r | bit].astype(jnp.float32) for r, v in blocks.items() if not r & bit}
+        bit *= 2
+    return blocks[0]
+
+
 def by_tokens(modded, targets, weights, capacity, experts, shards, sets):
     rows, width = modded.shape
     columns = width // shards
     slots = 2 * capacity
     me = lax.axis_index("expert")
+    mine = lax.axis_index("tensor")
     packed = jnp.concatenate((targets.astype(jnp.float32), weights), axis=1).T
-    routes = lax.all_gather(packed, "expert")
-    seen = lax.all_gather(modded, "expert")
-    local = routes[:, 0:2].astype(jnp.int32) - me * slots
-    number = jnp.arange(slots, dtype=jnp.int32)[None, :, None]
-    hits = [local[:, j][:, None, :] == number for j in range(2)]
-    pick = (hits[0] | hits[1]).astype(jnp.bfloat16)
-    factor = sum(
-        jnp.sum(jnp.where(hits[j], routes[:, 2 + j][:, None, :], 0.0), axis=2) for j in range(2)
-    )
-    hidden = []
-    for which, (gate, up, _) in enumerate(sets):
+    routes = gather_near(packed, "expert")
+    seen = gather_near(modded, "expert")
+    number = jnp.arange(slots, dtype=jnp.int32)[:, None]
+    pick, factor = {}, {}
+    for r, route in routes.items():
+        local = route[0:2].astype(jnp.int32) - me * slots
+        hits = [local[j][None, :] == number for j in range(2)]
+        pick[r] = (hits[0] | hits[1]).astype(jnp.bfloat16)
+        factor[r] = sum(
+            jnp.sum(jnp.where(hits[j], route[2 + j][None, :], 0.0), axis=1, keepdims=True)
+            for j in range(2)
+        )
+    order = sorted(seen)
+    served = {r: [] for r in order}
+    for which, (gate, up, down) in enumerate(sets):
         part = slice(which * capacity, (which + 1) * capacity)
-        arrived = lax.dot_general(
-            pick[:, part], seen, (((2,), (1,)), ((0,), (0,))), preferred_element_type=jnp.float32
-        ).astype(jnp.bfloat16)
-        hidden.append(hidden_of(arrived.reshape(experts * capacity, width), gate, up))
+        arrived = [dot32(pick[r][part], seen[r]).astype(jnp.bfloat16) for r in order]
+        hidden = hidden_of(jnp.concatenate(arrived, axis=0), gate, up)
+        scale = jnp.concatenate([factor[r][part] for r in order], axis=0)
+        out = (dot32(hidden, down) * scale).astype(jnp.bfloat16)
+        for at, r in enumerate(order):
+            served[r].append(out[at * capacity : (at + 1) * capacity])
+    served = {r: jnp.concatenate(v, axis=0) for r, v in served.items()}
     sums = []
-    step = columns // CHUNKS
+    step = rows // CHUNKS
     for c in range(CHUNKS):
-        done = []
-        for which, (_, _, down) in enumerate(sets):
-            piece = down.reshape(-1, shards, columns)[:, :, c * step : (c + 1) * step]
-            out = dot32(hidden[which], piece.reshape(-1, shards * step))
-            out = out.reshape(experts, capacity, shards * step)
-            scale = factor[:, which * capacity : (which + 1) * capacity]
-            done.append((out * scale[:, :, None]).astype(jnp.bfloat16))
-        served = jnp.concatenate(done, axis=1)
-        part = lax.dot_general(
-            pick, served, (((1,), (1,)), ((0,), (0,))), preferred_element_type=jnp.float32
-        ).astype(jnp.bfloat16)
-        own = lax.psum_scatter(
-            part.reshape(experts * rows, shards * step), "expert", scatter_dimension=0, tiled=True
-        )
-        sums.append(lax.psum_scatter(own, "tensor", scatter_dimension=1, tiled=True))
-    return jnp.concatenate(sums, axis=1).astype(jnp.float32)
+        terms = {
+            r: lax.dot_general(
+                pick[r][:, c * step : (c + 1) * step],
+                served[r],
+                (((0,), (0,)), ((), ())),
+                preferred_element_type=jnp.float32,
+            )
+            for r in order
+        }
+        own = reduce_near(terms, "expert")
+        split = {
+            r: lax.dynamic_slice_in_dim(own, (mine ^ r) * columns, columns, 1)
+            for r in range(shards)
+        }
+        sums.append(reduce_near(split, "tensor"))
+    return jnp.concatenate(sums, axis=0)
 
 
 def by_slots(modded, targets, weights, capacity, experts, shards, sets):
@@ -135,7 +166,8 @@
     modded = modulate(tokens.astype(jnp.float32), mod_row, width)
     targets = pair_targets(route_ids, partner, experts, capacity)
     sets = ((w_gate[0], w_up[0], w_down[0]), (spare_gate[0], spare_up[0], spare_down[0]))
-    plan = by_tokens if 2 * capacity >= rows else by_slots
+    paired = experts & (experts - 1) == 0 and shards & (shards - 1) == 0
+    plan = by_tokens if paired and 2 * capacity >= rows else by_slots
     mixed = plan(modded, targets, route_weights, capacity, experts, shards, sets)
     own_cols = lax.dynamic_slice_in_dim(tokens, tensor_start, columns, 1).astype(jnp.float32)
     gate_cols = lax.dynamic_slice_in_dim(mod_row, 2 * width + tensor_start, columns, 0)

time: 196 us -> 126 us (0.64)
  waiting for transfers between devices: 100 us -> 53.8 us
  local copies, waits for them, and re-layouts: 42 us -> 5.75 us
  starting transfers between devices: 0.17 us -> 15.6 us
  matrix products: 25.6 us -> 40.9 us
  between operations: 13.5 us -> 0.54 us
  blocking collectives: 6.38 us -> 0 us
  other arithmetic: 7.18 us -> 9.41 us
    reduce_scatter x4 -> x0, waiting for transfers between devices: 99.9 us -> none  [the longest x2 54.1 us: by_tokens(): lax.psum_scatter(part.reshape(experts * rows, shards * step), 'expert', s...]
    ppermute x0 -> x18, waiting for transfers between devices: none -> 53.8 us  [swap(): return lax.ppermute(value, axis, [(i, i ^ bit) for i in range(count)])]
    dot_general x9 -> x13, matrix products: 17.3 us -> 38 us  [dot32(): return jnp.dot(a, b, preferred_element_type=jnp.float32)]
    another operation x2 -> x0, local copies, waits for them, and re-layouts: 15.8 us -> none  [by_tokens(): piece = down.reshape(-1, shards, columns)[:, :, c * step:(c + 1) * step]]
    ppermute x0 -> x18, starting transfers between devices: none -> 15.6 us  [swap(): return lax.ppermute(value, axis, [(i, i ^ bit) for i in range(count)])]
    reshape x4 -> x0, local copies, waits for them, and re-layouts: 14.9 us -> none  [by_tokens(): out = dot32(hidden[which], piece.reshape(-1, shards * step))]
    all_gather x1 -> x0, blocking collectives: 6.38 us -> none  [by_tokens(): routes = lax.all_gather(packed, 'expert')]
    dot_general x4 -> x8, matrix products: 8.37 us -> 2.87 us  [by_tokens(): lax.dot_general(pick[r][:, c * step:(c + 1) * step], served[r], (((0,), (...]
  transfers between devices with their start and end apart: 5 -> 18, of which waited for: 4 -> 6; matrix products, arithmetic and copies ran while one was open for 24% -> 12% of each run, Pallas kernels for 0% -> 0%
where the time goes in v2:
time: 126 us
  waiting for transfers between devices  53.8 us (43%)
  matrix products  40.9 us (32%)
  starting transfers between devices  15.6 us (12%)
  other arithmetic  9.41 us (7%)
  local copies, waits for them, and re-layouts  5.75 us (5%)
    ppermute x18, waiting for transfers between devices, swap(): return lax.ppermute(value, axis, [(i, i ^ bit) for i in range(count)])  53.8 us
    dot_general x13, matrix products, dot32(): return jnp.dot(a, b, preferred_element_type=jnp.float32)  38 us
    ppermute x18, starting transfers between devices, swap(): return lax.ppermute(value, axis, [(i, i ^ bit) for i in range(count)])  15.6 us
    slice x2, local copies, waits for them, and re-layouts, by_tokens(): served[r].append(out[at * capacity:(at + 1) * capacity])  4.57 us
    dot_general x8, matrix products, by_tokens(): lax.dot_general(pick[r][:, c * step:(c + 1) * step], served[r], (((0,), (...  2.87 us
  transfers between devices with their start and end apart: 18, of which 6 were waited for; matrix products, arithmetic and copies ran while one was open for 12% of the time, Pallas kernels for 0%

profile of v2, /device:TPU:0, one launch (start us, length us, event | category | flops | bytes accessed | tf_op | source)
XLA Modules:
  0.0 126.0 jit_solution(14225943532646813599)
XLA Ops:
  3.8 2.9 %collective-permute-start.2 = (f32[4,256]{1,0:T(4,128)S(1)}, f32[4,256]{1,0:T(4,128)S(1)}, u32[]{:S(2)}, u32[]{:S(2)}) collective-permute-start(f32[4,256]{1,0:T(4,128)S(1)} %maximum_bitcast_fusion), channel_id=1, source_target_pairs={{0,8},{4,12},{8,0},{12,4},{1,9},{5,13},{9,1},{13,5},{2,10},{6,14},... | collective-permute-start | bytes 12296 | tf_op jit(solution)/shard_map/ppermute | solution.py:41
  6.7 1.4 %convert_reduce_fusion = f32[256]{0:T(256)S(1)} fusion(bf16[256,2048]{1,0:T(8,128)(2,1)} %param.11), kind=kLoop, calls=%fused_computation.15 | loop fusion | flops 1048320 | bytes 1049600 | tf_op jit(solution)/shard_map/reduce_sum | solution.py:28
  8.2 1.6 %fusion.18 = f32[256]{0:T(256)S(1)} fusion(bf16[256,2048]{1,0:T(8,128)(2,1)} %param.11, f32[256]{0:T(256)S(1)} %broadcast_multiply_fusion), kind=kLoop, calls=%fused_computation.30 | loop fusion | flops 2096896 | bytes 1050624 | tf_op jit(solution)/shard_map/reduce_sum | solution.py:30
  11.1 1.1 convolution_convert_fusion.7
  12.2 1.1 convolution_convert_fusion.11
  15.6 20.4 %collective-permute-done.3 = bf16[256,2048]{1,0:T(8,128)(2,1)S(1)} collective-permute-done((bf16[256,2048]{1,0:T(8,128)(2,1)S(1)}, bf16[256,2048]{1,0:T(8,128)(2,1)S(1)}, u32[]{:S(2)}, u32[]{:S(2)}) %collective-permute-start.3) | collective-permute-done | bytes 1048608 | tf_op jit(solution)/shard_map/ppermute | solution.py:41
  36.0 1.1 convolution_convert_fusion.5
  37.5 1.8 %convolution_convert_fusion.6 = bf16[128,2048]{1,0:T(8,128)(2,1)S(1)} fusion(bf16[256,2048]{1,0:T(8,128)(2,1)} %collective-permute-done.1, pred[256,256]{1,0:T(32,128)(4,1)S(1)} %fusion.38), kind=kOutput, calls=%fused_computation.24 | convolution fusion | flops 134479872 | bytes 1605632 | tf_op jit(solution)/shard_map/dot_general | solution.py:11
  39.2 1.7 %convolution_convert_fusion.10 = bf16[128,2048]{1,0:T(8,128)(2,1)S(1)} fusion(bf16[256,2048]{1,0:T(8,128)(2,1)} %collective-permute-done.1, pred[256,256]{1,0:T(32,128)(4,1)S(1)} %fusion.38), kind=kOutput, calls=%fused_computation.28 | convolution fusion | flops 134479872 | bytes 1605632 | tf_op jit(solution)/shard_map/dot_general | solution.py:11
  42.2 3.7 %fusion.10 = f32[512,1024]{1,0:T(8,128)} fusion(bf16[1,2048,1024]{2,1,0:T(8,128)(2,1)S(1)} %copy-done.13, bf16[128,2048]{1,0:T(8,128)(2,1)S(1)} %convolution_convert_fusion.8, bf16[128,2048]{1,0:T(8,128)(2,1)S(1)} %convolution_convert_fusion.9, bf16[128,2048]{1,0:T(8,128)(2,1)S(1)} %convolution_convert_fusion.10, bf16[128,2048]{1,0:T(8,128)(2,1)S(1)} %copy-done.4), kind=kOutput, calls=%fused_computation.10 | convolution fusion | flops 2155872256 | bytes 8388608 | tf_op jit(solution)/shard_map/dot_general | solution.py:11
  45.9 10.1 %multiply_convert_fusion.1 = bf16[512,2048]{1,0:T(8,128)(2,1)} fusion(bf16[1,1024,2048]{2,1,0:T(8,128)(2,1)} %param.18, f32[512]{0:T(512)S(1)} %bitcast.108, f32[512,1024]{1,0:T(8,128)} %fusion.10, bf16[1,2048,1024]{2,1,0:T(8,128)(2,1)} %param.17, bf16[128,2048]{1,0:T(8,128)(2,1)S(1)} %convolution_convert_fusion.8, bf16[128,2048]{1,0:T(8,128)(2,1)} %copy-done.7, ...), kind=kOutput, calls=%fused_computation.13 | convolution fusion | flops 4308598784 | bytes 14682112 | tf_op jit(solution)/shard_map/dot_general | solution.py:11
  56.1 2.9 %fusion.84 = (bf16[128,2048]{1,0:T(8,128)(2,1)}, bf16[128,2048]{1,0:T(8,128)(2,1)}, bf16[128,2048]{1,0:T(8,128)(2,1)}, bf16[128,2048]{1,0:T(8,128)(2,1)S(1)}) fusion(bf16[512,2048]{1,0:T(8,128)(2,1)} %multiply_convert_fusion.1), kind=kLoop, calls=%fused_computation.147 | loop fusion | bytes 4194304 | tf_op jit(solution)/shard_map/slice | solution.py:90
  59.3 6.2 %fusion.4 = f32[512,1024]{1,0:T(8,128)} fusion(bf16[1,2048,1024]{2,1,0:T(8,128)(2,1)} %param.19, bf16[128,2048]{1,0:T(8,128)(2,1)S(1)} %convolution_convert_fusion.4, bf16[128,2048]{1,0:T(8,128)(2,1)S(1)} %copy-done.6, bf16[128,2048]{1,0:T(8,128)(2,1)S(1)} %convolution_convert_fusion.6, bf16[128,2048]{1,0:T(8,128)(2,1)S(1)} %copy-done.3), kind=kOutput, calls=%fused_computation.4 | convolution fusion | flops 2155872256 | bytes 8388608 | tf_op jit(solution)/shard_map/dot_general | solution.py:11
  65.5 10.1 %multiply_convert_fusion = bf16[512,2048]{1,0:T(8,128)(2,1)} fusion(bf16[1,1024,2048]{2,1,0:T(8,128)(2,1)} %param.21, f32[512]{0:T(512)S(1)} %bitcast.107, f32[512,1024]{1,0:T(8,128)} %fusion.4, bf16[1,2048,1024]{2,1,0:T(8,128)(2,1)} %param.20, bf16[128,2048]{1,0:T(8,128)(2,1)} %copy-done.8, bf16[128,2048]{1,0:T(8,128)(2,1)S(1)} %copy-done.6, ...), kind=kOutput, calls=%fused_computation.12 | convolution fusion | flops 4308598784 | bytes 14682112 | tf_op jit(solution)/shard_map/dot_general | solution.py:11
  75.6 1.7 %fusion.85 = (bf16[128,2048]{1,0:T(8,128)(2,1)S(1)}, bf16[128,2048]{1,0:T(8,128)(2,1)S(1)}, bf16[128,2048]{1,0:T(8,128)(2,1)S(1)}, bf16[128,2048]{1,0:T(8,128)(2,1)S(1)}) fusion(bf16[512,2048]{1,0:T(8,128)(2,1)} %multiply_convert_fusion), kind=kLoop, calls=%fused_computation.148 | loop fusion | bytes 4194304 | tf_op jit(solution)/shard_map/slice | solution.py:90
  81.9 1.8 %collective-permute-start.14 = (bf16[128,2048]{1,0:T(8,128)(2,1)S(1)}, bf16[128,2048]{1,0:T(8,128)(2,1)S(1)}, u32[]{:S(2)}, u32[]{:S(2)}) collective-permute-start(bf16[128,2048]{1,0:T(8,128)(2,1)S(1)} %add_convert_fusion), channel_id=1, source_target_pairs={{0,8},{4,12},{8,0},{12,4},{1,9},{5,13},{9,1},{13,5},{2,10},{6,14},... | collective-permute-start | bytes 1572872 | tf_op jit(solution)/shard_map/ppermute | solution.py:41
  83.7 11.5 %collective-permute-done.8 = bf16[128,2048]{1,0:T(8,128)(2,1)S(1)} collective-permute-done((bf16[128,2048]{1,0:T(8,128)(2,1)S(1)}, bf16[128,2048]{1,0:T(8,128)(2,1)S(1)}, u32[]{:S(2)}, u32[]{:S(2)}) %collective-permute-start.8) | collective-permute-done | bytes 524320 | tf_op jit(solution)/shard_map/ppermute | solution.py:41
  95.5 1.7 %collective-permute-start.9 = (bf16[128,512]{1,0:T(8,128)(2,1)S(1)}, bf16[128,512]{1,0:T(8,128)(2,1)S(1)}, u32[]{:S(2)}, u32[]{:S(2)}) collective-permute-start(bf16[128,512]{1,0:T(8,128)(2,1)S(1)} %get-tuple-element.15), channel_id=1, source_target_pairs={{0,1},{1,0},{2,3},{3,2},{4,5},{5,4},{6,7},{7,6},{8,9},{9,8},{10,11... | collective-permute-start | bytes 393224 | tf_op jit(solution)/shard_map/ppermute | solution.py:41
  97.6 8.5 %collective-permute-done.14 = bf16[128,2048]{1,0:T(8,128)(2,1)S(1)} collective-permute-done((bf16[128,2048]{1,0:T(8,128)(2,1)S(1)}, bf16[128,2048]{1,0:T(8,128)(2,1)S(1)}, u32[]{:S(2)}, u32[]{:S(2)}) %collective-permute-start.14) | collective-permute-done | bytes 524320 | tf_op jit(solution)/shard_map/ppermute | solution.py:41
  106.3 1.7 %collective-permute-start.15 = (bf16[128,512]{1,0:T(8,128)(2,1)S(1)}, bf16[128,512]{1,0:T(8,128)(2,1)S(1)}, u32[]{:S(2)}, u32[]{:S(2)}) collective-permute-start(bf16[128,512]{1,0:T(8,128)(2,1)S(1)} %get-tuple-element.17), channel_id=1, source_target_pairs={{0,1},{1,0},{2,3},{3,2},{4,5},{5,4},{6,7},{7,6},{8,9},{9,8},{10,11... | collective-permute-start | bytes 393224 | tf_op jit(solution)/shard_map/ppermute | solution.py:41
  108.5 2.6 %collective-permute-start.11 = (bf16[128,512]{1,0:T(8,128)(2,1)S(1)}, bf16[128,512]{1,0:T(8,128)(2,1)S(1)}, u32[]{:S(2)}, u32[]{:S(2)}) collective-permute-start(bf16[128,512]{1,0:T(8,128)(2,1)S(1)} %add_convert_fusion.3), channel_id=1, source_target_pairs={{0,2},{1,3},{2,0},{3,1},{4,6},{5,7},{6,4},{7,5},{8,10},{9,11},{10,... | collective-permute-start | bytes 393224 | tf_op jit(solution)/shard_map/ppermute | solution.py:41
  111.1 6.0 %collective-permute-done.16 = bf16[128,512]{1,0:T(8,128)(2,1)S(1)} collective-permute-done((bf16[128,512]{1,0:T(8,128)(2,1)S(1)}, bf16[128,512]{1,0:T(8,128)(2,1)S(1)}, u32[]{:S(2)}, u32[]{:S(2)}) %collective-permute-start.16) | collective-permute-done | bytes 131104 | tf_op jit(solution)/shard_map/ppermute | solution.py:41
  117.1 1.6 %collective-permute-start.17 = (bf16[128,512]{1,0:T(8,128)(2,1)S(1)}, bf16[128,512]{1,0:T(8,128)(2,1)S(1)}, u32[]{:S(2)}, u32[]{:S(2)}) collective-permute-start(bf16[128,512]{1,0:T(8,128)(2,1)S(1)} %add_convert_fusion.2), channel_id=1, source_target_pairs={{0,2},{1,3},{2,0},{3,1},{4,6},{5,7},{6,4},{7,5},{8,10},{9,11},{10,... | collective-permute-start | bytes 393224 | tf_op jit(solution)/shard_map/ppermute | solution.py:41
  118.9 6.3 %collective-permute-done.17 = bf16[128,512]{1,0:T(8,128)(2,1)S(1)} collective-permute-done((bf16[128,512]{1,0:T(8,128)(2,1)S(1)}, bf16[128,512]{1,0:T(8,128)(2,1)S(1)}, u32[]{:S(2)}, u32[]{:S(2)}) %collective-permute-start.17) | collective-permute-done | bytes 131104 | tf_op jit(solution)/shard_map/ppermute | solution.py:41
  (114 shorter events, 15.9 us)
Async XLA Ops:
  0.0 9.9 %copy-start = (bf16[256,2048]{1,0:T(8,128)(2,1)S(1)}, bf16[256,2048]{1,0:T(8,128)(2,1)}, u32[]{:S(2)}) copy-start(bf16[256,2048]{1,0:T(8,128)(2,1)} %param.11) | copy-start | bytes 3145732
  0.0 9.8 %copy-start.12 = (f32[1,6144]{1,0:T(1,128)S(1)}, f32[1,6144]{1,0:T(1,128)}, u32[]{:S(2)}) copy-start(f32[1,6144]{1,0:T(1,128)} %param.14) | copy-start | bytes 73732
  3.8 9.8 %collective-permute-start.2 = (f32[4,256]{1,0:T(4,128)S(1)}, f32[4,256]{1,0:T(4,128)S(1)}, u32[]{:S(2)}, u32[]{:S(2)}) collective-permute-start(f32[4,256]{1,0:T(4,128)S(1)} %maximum_bitcast_fusion), channel_id=1, source_target_pairs={{0,8},{4,12},{8,0},{12,4},{1,9},{5,13},{9,1},{13,5},{2,10},{6,14},... | collective-permute-start | bytes 12296 | tf_op jit(solution)/shard_map/ppermute | solution.py:41
  6.7 7.1 %collective-permute-start = (f32[4,256]{1,0:T(4,128)S(1)}, f32[4,256]{1,0:T(4,128)S(1)}, u32[]{:S(2)}, u32[]{:S(2)}) collective-permute-start(f32[4,256]{1,0:T(4,128)S(1)} %maximum_bitcast_fusion), channel_id=1, source_target_pairs={{0,4},{4,0},{8,12},{12,8},{1,5},{5,1},{9,13},{13,9},{2,6},{6,2},{1... | collective-permute-start | bytes 12296 | tf_op jit(solution)/shard_map/ppermute | solution.py:41
  10.3 25.6 %collective-permute-start.3 = (bf16[256,2048]{1,0:T(8,128)(2,1)S(1)}, bf16[256,2048]{1,0:T(8,128)(2,1)S(1)}, u32[]{:S(2)}, u32[]{:S(2)}) collective-permute-start(bf16[256,2048]{1,0:T(8,128)(2,1)S(1)} %fusion.21), channel_id=1, source_target_pairs={{0,8},{4,12},{8,0},{12,4},{1,9},{5,13},{9,1},{13,5},{2,10},{6,14},... | collective-permute-start | bytes 3145736 | tf_op jit(solution)/shard_map/ppermute | solution.py:41
  10.5 27.0 %collective-permute-start.1 = (bf16[256,2048]{1,0:T(8,128)(2,1)S(1)}, bf16[256,2048]{1,0:T(8,128)(2,1)}, u32[]{:S(2)}, u32[]{:S(2)}) collective-permute-start(bf16[256,2048]{1,0:T(8,128)(2,1)S(1)} %fusion.21), channel_id=1, source_target_pairs={{0,4},{4,0},{8,12},{12,8},{1,5},{5,1},{9,13},{13,9},{2,6},{6,2},{1... | collective-permute-start | bytes 3145736 | tf_op jit(solution)/shard_map/ppermute | solution.py:41
  14.1 1.2 collective-permute-start.4
  36.0 4.9 %collective-permute-start.5 = (bf16[256,2048]{1,0:T(8,128)(2,1)S(1)}, bf16[256,2048]{1,0:T(8,128)(2,1)S(1)}, u32[]{:S(2)}, u32[]{:S(2)}) collective-permute-start(bf16[256,2048]{1,0:T(8,128)(2,1)S(1)} %collective-permute-done.3), channel_id=1, source_target_pairs={{0,4},{4,0},{8,12},{12,8},{1,5},{5,1},{9,13},{13,9},{2,6},{6,2},{1... | collective-permute-start | bytes 3145736 | tf_op jit(solution)/shard_map/ppermute | solution.py:41
  37.4 4.8 %copy-start.7 = (bf16[128,2048]{1,0:T(8,128)(2,1)}, bf16[128,2048]{1,0:T(8,128)(2,1)S(1)}, u32[]{:S(2)}) copy-start(bf16[128,2048]{1,0:T(8,128)(2,1)S(1)} %convolution_convert_fusion.9) | copy-start | bytes 1572868
  37.4 4.8 %copy-start.4 = (bf16[128,2048]{1,0:T(8,128)(2,1)S(1)}, bf16[128,2048]{1,0:T(8,128)(2,1)}, u32[]{:S(2)}) copy-start(bf16[128,2048]{1,0:T(8,128)(2,1)} %convolution_convert_fusion.11) | copy-start | bytes 1572868
  37.4 4.8 %copy-start.13 = (bf16[1,2048,1024]{2,1,0:T(8,128)(2,1)S(1)}, bf16[1,2048,1024]{2,1,0:T(8,128)(2,1)}, u32[]{:S(2)}) copy-start(bf16[1,2048,1024]{2,1,0:T(8,128)(2,1)} %param.16) | copy-start | bytes 12582916
  59.3 6.2 %copy-start.8 = (bf16[128,2048]{1,0:T(8,128)(2,1)}, bf16[128,2048]{1,0:T(8,128)(2,1)S(1)}, u32[]{:S(2)}) copy-start(bf16[128,2048]{1,0:T(8,128)(2,1)S(1)} %convolution_convert_fusion.4) | copy-start | bytes 1572868
  77.7 2.4 %collective-permute-start.7 = (bf16[128,2048]{1,0:T(8,128)(2,1)S(1)}, bf16[128,2048]{1,0:T(8,128)(2,1)S(1)}, u32[]{:S(2)}, u32[]{:S(2)}) collective-permute-start(bf16[128,2048]{1,0:T(8,128)(2,1)S(1)} %convolution_convert_fusion.2), channel_id=1, source_target_pairs={{0,4},{4,0},{8,12},{12,8},{1,5},{5,1},{9,13},{13,9},{2,6},{6,2},{1... | collective-permute-start | bytes 1572872 | tf_op jit(solution)/shard_map/ppermute | solution.py:41
  78.6 2.9 %collective-permute-start.13 = (bf16[128,2048]{1,0:T(8,128)(2,1)S(1)}, bf16[128,2048]{1,0:T(8,128)(2,1)S(1)}, u32[]{:S(2)}, u32[]{:S(2)}) collective-permute-start(bf16[128,2048]{1,0:T(8,128)(2,1)S(1)} %convolution_convert_fusion), channel_id=1, source_target_pairs={{0,4},{4,0},{8,12},{12,8},{1,5},{5,1},{9,13},{13,9},{2,6},{6,2},{1... | collective-permute-start | bytes 1572872 | tf_op jit(solution)/shard_map/ppermute | solution.py:41
  79.1 4.6 %collective-permute-start.6 = (bf16[128,2048]{1,0:T(8,128)(2,1)S(1)}, bf16[128,2048]{1,0:T(8,128)(2,1)S(1)}, u32[]{:S(2)}, u32[]{:S(2)}) collective-permute-start(bf16[128,2048]{1,0:T(8,128)(2,1)S(1)} %convolution_convert_fusion.3), channel_id=1, source_target_pairs={{0,4},{4,0},{8,12},{12,8},{1,5},{5,1},{9,13},{13,9},{2,6},{6,2},{1... | collective-permute-start | bytes 1572872 | tf_op jit(solution)/shard_map/ppermute | solution.py:41
  80.0 17.6 %collective-permute-start.12 = (bf16[128,2048]{1,0:T(8,128)(2,1)S(1)}, bf16[128,2048]{1,0:T(8,128)(2,1)S(1)}, u32[]{:S(2)}, u32[]{:S(2)}) collective-permute-start(bf16[128,2048]{1,0:T(8,128)(2,1)S(1)} %convolution_convert_fusion.1), channel_id=1, source_target_pairs={{0,4},{4,0},{8,12},{12,8},{1,5},{5,1},{9,13},{13,9},{2,6},{6,2},{1... | collective-permute-start | bytes 1572872 | tf_op jit(solution)/shard_map/ppermute | solution.py:41
  80.5 14.8 %collective-permute-start.8 = (bf16[128,2048]{1,0:T(8,128)(2,1)S(1)}, bf16[128,2048]{1,0:T(8,128)(2,1)S(1)}, u32[]{:S(2)}, u32[]{:S(2)}) collective-permute-start(bf16[128,2048]{1,0:T(8,128)(2,1)S(1)} %add_convert_fusion.1), channel_id=1, source_target_pairs={{0,8},{4,12},{8,0},{12,4},{1,9},{5,13},{9,1},{13,5},{2,10},{6,14},... | collective-permute-start | bytes 1572872 | tf_op jit(solution)/shard_map/ppermute | solution.py:41
  81.9 24.2 %collective-permute-start.14 = (bf16[128,2048]{1,0:T(8,128)(2,1)S(1)}, bf16[128,2048]{1,0:T(8,128)(2,1)S(1)}, u32[]{:S(2)}, u32[]{:S(2)}) collective-permute-start(bf16[128,2048]{1,0:T(8,128)(2,1)S(1)} %add_convert_fusion), channel_id=1, source_target_pairs={{0,8},{4,12},{8,0},{12,4},{1,9},{5,13},{9,1},{13,5},{2,10},{6,14},... | collective-permute-start | bytes 1572872 | tf_op jit(solution)/shard_map/ppermute | solution.py:41
  95.5 23.3 %collective-permute-start.9 = (bf16[128,512]{1,0:T(8,128)(2,1)S(1)}, bf16[128,512]{1,0:T(8,128)(2,1)S(1)}, u32[]{:S(2)}, u32[]{:S(2)}) collective-permute-start(bf16[128,512]{1,0:T(8,128)(2,1)S(1)} %get-tuple-element.15), channel_id=1, source_target_pairs={{0,1},{1,0},{2,3},{3,2},{4,5},{5,4},{6,7},{7,6},{8,9},{9,8},{10,11... | collective-permute-start | bytes 393224 | tf_op jit(solution)/shard_map/ppermute | solution.py:41
  97.2 11.2 %collective-permute-start.10 = (bf16[128,512]{1,0:T(8,128)(2,1)S(1)}, bf16[128,512]{1,0:T(8,128)(2,1)S(1)}, u32[]{:S(2)}, u32[]{:S(2)}) collective-permute-start(bf16[128,512]{1,0:T(8,128)(2,1)S(1)} %get-tuple-element.16), channel_id=1, source_target_pairs={{0,1},{1,0},{2,3},{3,2},{4,5},{5,4},{6,7},{7,6},{8,9},{9,8},{10,11... | collective-permute-start | bytes 393224 | tf_op jit(solution)/shard_map/ppermute | solution.py:41
  106.3 12.5 %collective-permute-start.15 = (bf16[128,512]{1,0:T(8,128)(2,1)S(1)}, bf16[128,512]{1,0:T(8,128)(2,1)S(1)}, u32[]{:S(2)}, u32[]{:S(2)}) collective-permute-start(bf16[128,512]{1,0:T(8,128)(2,1)S(1)} %get-tuple-element.17), channel_id=1, source_target_pairs={{0,1},{1,0},{2,3},{3,2},{4,5},{5,4},{6,7},{7,6},{8,9},{9,8},{10,11... | collective-permute-start | bytes 393224 | tf_op jit(solution)/shard_map/ppermute | solution.py:41
  108.0 9.1 %collective-permute-start.16 = (bf16[128,512]{1,0:T(8,128)(2,1)S(1)}, bf16[128,512]{1,0:T(8,128)(2,1)S(1)}, u32[]{:S(2)}, u32[]{:S(2)}) collective-permute-start(bf16[128,512]{1,0:T(8,128)(2,1)S(1)} %get-tuple-element.18), channel_id=1, source_target_pairs={{0,1},{1,0},{2,3},{3,2},{4,5},{5,4},{6,7},{7,6},{8,9},{9,8},{10,11... | collective-permute-start | bytes 393224 | tf_op jit(solution)/shard_map/ppermute | solution.py:41
  108.5 10.3 %collective-permute-start.11 = (bf16[128,512]{1,0:T(8,128)(2,1)S(1)}, bf16[128,512]{1,0:T(8,128)(2,1)S(1)}, u32[]{:S(2)}, u32[]{:S(2)}) collective-permute-start(bf16[128,512]{1,0:T(8,128)(2,1)S(1)} %add_convert_fusion.3), channel_id=1, source_target_pairs={{0,2},{1,3},{2,0},{3,1},{4,6},{5,7},{6,4},{7,5},{8,10},{9,11},{10,... | collective-permute-start | bytes 393224 | tf_op jit(solution)/shard_map/ppermute | solution.py:41
  117.1 8.0 %collective-permute-start.17 = (bf16[128,512]{1,0:T(8,128)(2,1)S(1)}, bf16[128,512]{1,0:T(8,128)(2,1)S(1)}, u32[]{:S(2)}, u32[]{:S(2)}) collective-permute-start(bf16[128,512]{1,0:T(8,128)(2,1)S(1)} %add_convert_fusion.2), channel_id=1, source_target_pairs={{0,2},{1,3},{2,0},{3,1},{4,6},{5,7},{6,4},{7,5},{8,10},{9,11},{10,... | collective-permute-start | bytes 393224 | tf_op jit(solution)/shard_map/ppermute | solution.py:41
  (8 other events, 18.5 us)

commit v3 on v2

--- a/solution.py
+++ b/solution.py
@@ -33,7 +33,8 @@
 
 
 def hidden_of(rows, gate, up):
-    return (jax.nn.silu(dot32(rows, gate)) * dot32(rows, up)).astype(jnp.bfloat16)
+    gated, raised = lax.optimization_barrier((dot32(rows, gate), dot32(rows, up)))
+    return (jax.nn.silu(gated) * raised).astype(jnp.bfloat16)
 
 
 def swap(value, axis, bit):
@@ -80,14 +81,16 @@
         )
     order = sorted(seen)
     served = {r: [] for r in order}
-    for which, (gate, up, down) in enumerate(sets):
-        part = slice(which * capacity, (which + 1) * capacity)
-        arrived = [dot32(pick[r][part], seen[r]).astype(jnp.bfloat16) for r in order]
-        hidden = hidden_of(jnp.concatenate(arrived, axis=0), gate, up)
-        scale = jnp.concatenate([factor[r][part] for r in order], axis=0)
-        out = (dot32(hidden, down) * scale).astype(jnp.bfloat16)
-        for at, r in enumerate(order):
-            served[r].append(out[at * capacity : (at + 1) * capacity])
+    near = max(1, experts // 2)
+    for group in (order[:near], order[near:]):
+        for which, (gate, up, down) in enumerate(sets if group else ()):
+            part = slice(which * capacity, (which + 1) * capacity)
+            arrived = [dot32(pick[r][part], seen[r]).astype(jnp.bfloat16) for r in group]
+            hidden = hidden_of(jnp.concatenate(arrived, axis=0), gate, up)
+            scale = jnp.concatenate([factor[r][part] for r in group], axis=0)
+            out = (dot32(hidden, down) * scale).astype(jnp.bfloat16)
+            for at, r in enumerate(group):
+                served[r].append(out[at * capacity : (at + 1) * capacity])
     served = {r: jnp.concatenate(v, axis=0) for r, v in served.items()}
     sums = []
     step = rows // CHUNKS

time: 126 us -> 96.1 us (0.76)
  waiting for transfers between devices: 53.8 us -> 40.2 us
  matrix products: 40.9 us -> 28 us
  local copies, waits for them, and re-layouts: 5.75 us -> 2.33 us
    ppermute x18, waiting for transfers between devices: 53.8 us -> 40.2 us  [swap(): return lax.ppermute(value, axis, [(i, i ^ bit) for i in range(count)])]
    dot_general x13 -> x21, matrix products: 38 us -> 25.1 us  [dot32(): return jnp.dot(a, b, preferred_element_type=jnp.float32)]
    slice x2 -> x4, local copies, waits for them, and re-layouts: 4.57 us -> 0.35 us  [by_tokens(): served[r].append(out[at * capacity:(at + 1) * capacity])]
  transfers between devices with their start and end apart: 18 -> 18, of which waited for: 6 -> 8; matrix products, arithmetic and copies ran while one was open for 12% -> 25% of each run, Pallas kernels for 0% -> 0%
where the time goes in v3:
time: 96.1 us; the launch traced here: 95.7 us
  waiting for transfers between devices  40.2 us (42%)
  matrix products  28 us (29%)
  starting transfers between devices  15.2 us (16%)
  other arithmetic  9.39 us (10%)
  local copies, waits for them, and re-layouts  2.33 us (2%)
    ppermute x18, waiting for transfers between devices, swap(): return lax.ppermute(value, axis, [(i, i ^ bit) for i in range(count)])  40.2 us
    dot_general x21, matrix products, dot32(): return jnp.dot(a, b, preferred_element_type=jnp.float32)  25.1 us
    ppermute x18, starting transfers between devices, swap(): return lax.ppermute(value, axis, [(i, i ^ bit) for i in range(count)])  15.2 us
    dot_general x8, matrix products, by_tokens(): lax.dot_general(pick[r][:, c * step:(c + 1) * step], served[r], (((0,), (...  2.86 us
  transfers between devices with their start and end apart: 18, of which 8 were waited for; matrix products, arithmetic and copies ran while one was open for 25% of the time, Pallas kernels for 0%

profile of v3, /device:TPU:0, one launch (start us, length us, event | category | flops | bytes accessed | tf_op | source)
XLA Modules:
  0.0 95.7 jit_solution(18237556749526505087)
XLA Ops:
  3.8 2.9 %collective-permute-start.3 = (f32[4,256]{1,0:T(4,128)S(1)}, f32[4,256]{1,0:T(4,128)S(1)}, u32[]{:S(2)}, u32[]{:S(2)}) collective-permute-start(f32[4,256]{1,0:T(4,128)S(1)} %maximum_bitcast_fusion), channel_id=1, source_target_pairs={{0,8},{4,12},{8,0},{12,4},{1,9},{5,13},{9,1},{13,5},{2,10},{6,14},... | collective-permute-start | bytes 12296 | tf_op jit(solution)/shard_map/ppermute | solution.py:42
  6.7 1.4 %convert_reduce_fusion = f32[256]{0:T(256)S(1)} fusion(bf16[256,2048]{1,0:T(8,128)(2,1)} %param.11), kind=kLoop, calls=%fused_computation.29 | loop fusion | flops 1048320 | bytes 1049600 | tf_op jit(solution)/shard_map/reduce_sum | solution.py:28
  8.2 1.6 %fusion.50 = f32[256]{0:T(256)S(1)} fusion(bf16[256,2048]{1,0:T(8,128)(2,1)} %param.11, f32[256]{0:T(256)S(1)} %broadcast_multiply_fusion), kind=kLoop, calls=%fused_computation.48 | loop fusion | flops 2096896 | bytes 1050624 | tf_op jit(solution)/shard_map/reduce_sum | solution.py:30
  15.6 1.5 %convolution_convert_fusion.10 = bf16[128,2048]{1,0:T(8,128)(2,1)S(1)} fusion(bf16[256,2048]{1,0:T(8,128)(2,1)} %collective-permute-done.1, pred[256,256]{1,0:T(32,128)(4,1)S(1)} %fusion.66), kind=kOutput, calls=%fused_computation.46 | convolution fusion | flops 134479872 | bytes 1605632 | tf_op jit(solution)/shard_map/dot_general | solution.py:11
  17.2 3.7 %fusion.18 = f32[256,1024]{1,0:T(8,128)S(1)} fusion(bf16[1,2048,1024]{2,1,0:T(8,128)(2,1)} %param.17, bf16[128,2048]{1,0:T(8,128)(2,1)S(1)} %convolution_convert_fusion.10, bf16[128,2048]{1,0:T(8,128)(2,1)} %convolution_convert_fusion.11), kind=kOutput, calls=%fused_computation.18 | convolution fusion | flops 1075838976 | bytes 6291456 | tf_op jit(solution)/shard_map/dot_general | solution.py:11
  22.3 1.6 %convolution_convert_fusion.8 = bf16[128,2048]{1,0:T(8,128)(2,1)S(1)} fusion(bf16[256,2048]{1,0:T(8,128)(2,1)} %collective-permute-done.1, pred[256,256]{1,0:T(32,128)(4,1)S(1)} %fusion.66), kind=kOutput, calls=%fused_computation.44 | convolution fusion | flops 134479872 | bytes 1605632 | tf_op jit(solution)/shard_map/dot_general | solution.py:11
  24.0 1.3 %fusion.6 = f32[256,1024]{1,0:T(8,128)S(1)} fusion(bf16[1,2048,1024]{2,1,0:T(8,128)(2,1)S(1)} %copy-done.6, bf16[128,2048]{1,0:T(8,128)(2,1)S(1)} %convolution_convert_fusion.8, bf16[128,2048]{1,0:T(8,128)(2,1)S(1)} %copy-done.1), kind=kOutput, calls=%fused_computation.6 | convolution fusion | flops 1075838976 | bytes 6291456 | tf_op jit(solution)/shard_map/dot_general | solution.py:11
  26.2 1.3 %fusion.10 = f32[256,1024]{1,0:T(8,128)S(1)} fusion(bf16[1,2048,1024]{2,1,0:T(8,128)(2,1)S(1)} %copy-done.7, bf16[128,2048]{1,0:T(8,128)(2,1)S(1)} %convolution_convert_fusion.8, bf16[128,2048]{1,0:T(8,128)(2,1)S(1)} %copy-done.1), kind=kOutput, calls=%fused_computation.10 | convolution fusion | flops 1075838976 | bytes 6291456 | tf_op jit(solution)/shard_map/dot_general | solution.py:11
  28.3 1.3 %fusion.45 = bf16[256,2048]{1,0:T(8,128)(2,1)S(1)} fusion(bf16[1,1024,2048]{2,1,0:T(8,128)(2,1)S(1)} %copy-done.8, f32[256]{0:T(256)S(1)} %bitcast.127, f32[256,1024]{1,0:T(8,128)S(1)} %fusion.18, f32[256,1024]{1,0:T(8,128)S(1)} %fusion.22), kind=kOutput, calls=%fused_computation.33 | convolution fusion | flops 1076363264 | bytes 7341056 | tf_op jit(solution)/shard_map/dot_general | solution.py:11
  29.8 6.2 %collective-permute-done.4 = bf16[256,2048]{1,0:T(8,128)(2,1)S(1)} collective-permute-done((bf16[256,2048]{1,0:T(8,128)(2,1)S(1)}, bf16[256,2048]{1,0:T(8,128)(2,1)S(1)}, u32[]{:S(2)}, u32[]{:S(2)}) %collective-permute-start.4) | collective-permute-done | bytes 1048608 | tf_op jit(solution)/shard_map/ppermute | solution.py:42
  36.6 1.3 %fusion.39 = bf16[256,2048]{1,0:T(8,128)(2,1)S(1)} fusion(bf16[1,1024,2048]{2,1,0:T(8,128)(2,1)S(1)} %copy-done.9, f32[256]{0:T(256)S(1)} %bitcast.125, f32[256,1024]{1,0:T(8,128)S(1)} %fusion.6, f32[256,1024]{1,0:T(8,128)S(1)} %fusion.10), kind=kOutput, calls=%fused_computation.31 | convolution fusion | flops 1076363264 | bytes 7341056 | tf_op jit(solution)/shard_map/dot_general | solution.py:11
  40.2 1.5 %fusion.20 = f32[256,1024]{1,0:T(8,128)S(1)} fusion(bf16[1,2048,1024]{2,1,0:T(8,128)(2,1)S(1)} %copy-done.5, bf16[128,2048]{1,0:T(8,128)(2,1)S(1)} %convolution_convert_fusion.5, bf16[128,2048]{1,0:T(8,128)(2,1)S(1)} %convolution_convert_fusion.6), kind=kOutput, calls=%fused_computation.20 | convolution fusion | flops 1075838976 | bytes 6291456 | tf_op jit(solution)/shard_map/dot_general | solution.py:11
  43.3 1.3 %fusion.8 = f32[256,1024]{1,0:T(8,128)S(1)} fusion(bf16[1,2048,1024]{2,1,0:T(8,128)(2,1)S(1)} %copy-done.7, bf16[128,2048]{1,0:T(8,128)(2,1)S(1)} %convolution_convert_fusion.3, bf16[128,2048]{1,0:T(8,128)(2,1)S(1)} %convolution_convert_fusion.4), kind=kOutput, calls=%fused_computation.8 | convolution fusion | flops 1075838976 | bytes 6291456 | tf_op jit(solution)/shard_map/dot_general | solution.py:11
  44.6 1.3 %fusion.42 = bf16[256,2048]{1,0:T(8,128)(2,1)S(1)} fusion(bf16[1,1024,2048]{2,1,0:T(8,128)(2,1)S(1)} %copy-done.8, f32[256]{0:T(256)S(1)} %bitcast.128, f32[256,1024]{1,0:T(8,128)S(1)} %fusion.16, f32[256,1024]{1,0:T(8,128)S(1)} %fusion.20), kind=kOutput, calls=%fused_computation.32 | convolution fusion | flops 1076363264 | bytes 7341056 | tf_op jit(solution)/shard_map/dot_general | solution.py:11
  46.0 1.3 %fusion.36 = bf16[256,2048]{1,0:T(8,128)(2,1)S(1)} fusion(bf16[1,1024,2048]{2,1,0:T(8,128)(2,1)S(1)} %copy-done.9, f32[256]{0:T(256)S(1)} %bitcast.126, f32[256,1024]{1,0:T(8,128)S(1)} %fusion.4, f32[256,1024]{1,0:T(8,128)S(1)} %fusion.8), kind=kOutput, calls=%fused_computation.30 | convolution fusion | flops 1076363264 | bytes 7341056 | tf_op jit(solution)/shard_map/dot_general | solution.py:11
  52.5 1.4 %collective-permute-start.14 = (bf16[128,2048]{1,0:T(8,128)(2,1)S(1)}, bf16[128,2048]{1,0:T(8,128)(2,1)S(1)}, u32[]{:S(2)}, u32[]{:S(2)}) collective-permute-start(bf16[128,2048]{1,0:T(8,128)(2,1)S(1)} %add_convert_fusion), channel_id=1, source_target_pairs={{0,8},{4,12},{8,0},{12,4},{1,9},{5,13},{9,1},{13,5},{2,10},{6,14},... | collective-permute-start | bytes 1572872 | tf_op jit(solution)/shard_map/ppermute | solution.py:42
  53.9 11.5 %collective-permute-done.8 = bf16[128,2048]{1,0:T(8,128)(2,1)S(1)} collective-permute-done((bf16[128,2048]{1,0:T(8,128)(2,1)S(1)}, bf16[128,2048]{1,0:T(8,128)(2,1)S(1)}, u32[]{:S(2)}, u32[]{:S(2)}) %collective-permute-start.8) | collective-permute-done | bytes 524320 | tf_op jit(solution)/shard_map/ppermute | solution.py:42
  65.7 1.6 %collective-permute-start.9 = (bf16[128,512]{1,0:T(8,128)(2,1)S(1)}, bf16[128,512]{1,0:T(8,128)(2,1)S(1)}, u32[]{:S(2)}, u32[]{:S(2)}) collective-permute-start(bf16[128,512]{1,0:T(8,128)(2,1)S(1)} %get-tuple-element.23), channel_id=1, source_target_pairs={{0,1},{1,0},{2,3},{3,2},{4,5},{5,4},{6,7},{7,6},{8,9},{9,8},{10,11... | collective-permute-start | bytes 393224 | tf_op jit(solution)/shard_map/ppermute | solution.py:42
  67.7 8.3 %collective-permute-done.14 = bf16[128,2048]{1,0:T(8,128)(2,1)S(1)} collective-permute-done((bf16[128,2048]{1,0:T(8,128)(2,1)S(1)}, bf16[128,2048]{1,0:T(8,128)(2,1)S(1)}, u32[]{:S(2)}, u32[]{:S(2)}) %collective-permute-start.14) | collective-permute-done | bytes 524320 | tf_op jit(solution)/shard_map/ppermute | solution.py:42
  76.3 1.6 %collective-permute-start.15 = (bf16[128,512]{1,0:T(8,128)(2,1)S(1)}, bf16[128,512]{1,0:T(8,128)(2,1)S(1)}, u32[]{:S(2)}, u32[]{:S(2)}) collective-permute-start(bf16[128,512]{1,0:T(8,128)(2,1)S(1)} %get-tuple-element.25), channel_id=1, source_target_pairs={{0,1},{1,0},{2,3},{3,2},{4,5},{5,4},{6,7},{7,6},{8,9},{9,8},{10,11... | collective-permute-start | bytes 393224 | tf_op jit(solution)/shard_map/ppermute | solution.py:42
  78.5 2.6 %collective-permute-start.11 = (bf16[128,512]{1,0:T(8,128)(2,1)S(1)}, bf16[128,512]{1,0:T(8,128)(2,1)S(1)}, u32[]{:S(2)}, u32[]{:S(2)}) collective-permute-start(bf16[128,512]{1,0:T(8,128)(2,1)S(1)} %add_convert_fusion.3), channel_id=1, source_target_pairs={{0,2},{1,3},{2,0},{3,1},{4,6},{5,7},{6,4},{7,5},{8,10},{9,11},{10,... | collective-permute-start | bytes 393224 | tf_op jit(solution)/shard_map/ppermute | solution.py:42
  81.1 5.9 %collective-permute-done.16 = bf16[128,512]{1,0:T(8,128)(2,1)S(1)} collective-permute-done((bf16[128,512]{1,0:T(8,128)(2,1)S(1)}, bf16[128,512]{1,0:T(8,128)(2,1)S(1)}, u32[]{:S(2)}, u32[]{:S(2)}) %collective-permute-start.16) | collective-permute-done | bytes 131104 | tf_op jit(solution)/shard_map/ppermute | solution.py:42
  87.0 1.6 %collective-permute-start.17 = (bf16[128,512]{1,0:T(8,128)(2,1)S(1)}, bf16[128,512]{1,0:T(8,128)(2,1)S(1)}, u32[]{:S(2)}, u32[]{:S(2)}) collective-permute-start(bf16[128,512]{1,0:T(8,128)(2,1)S(1)} %add_convert_fusion.2), channel_id=1, source_target_pairs={{0,2},{1,3},{2,0},{3,1},{4,6},{5,7},{6,4},{7,5},{8,10},{9,11},{10,... | collective-permute-start | bytes 393224 | tf_op jit(solution)/shard_map/ppermute | solution.py:42
  88.7 6.1 %collective-permute-done.17 = bf16[128,512]{1,0:T(8,128)(2,1)S(1)} collective-permute-done((bf16[128,512]{1,0:T(8,128)(2,1)S(1)}, bf16[128,512]{1,0:T(8,128)(2,1)S(1)}, u32[]{:S(2)}, u32[]{:S(2)}) %collective-permute-start.17) | collective-permute-done | bytes 131104 | tf_op jit(solution)/shard_map/ppermute | solution.py:42
  (118 shorter events, 24.4 us)
Async XLA Ops:
  0.0 9.9 %copy-start = (bf16[256,2048]{1,0:T(8,128)(2,1)S(1)}, bf16[256,2048]{1,0:T(8,128)(2,1)}, u32[]{:S(2)}) copy-start(bf16[256,2048]{1,0:T(8,128)(2,1)} %param.11) | copy-start | bytes 3145732
  0.0 9.8 %copy-start.3 = (f32[1,6144]{1,0:T(1,128)S(1)}, f32[1,6144]{1,0:T(1,128)}, u32[]{:S(2)}) copy-start(f32[1,6144]{1,0:T(1,128)} %param.14) | copy-start | bytes 73732
  3.8 9.8 %collective-permute-start.3 = (f32[4,256]{1,0:T(4,128)S(1)}, f32[4,256]{1,0:T(4,128)S(1)}, u32[]{:S(2)}, u32[]{:S(2)}) collective-permute-start(f32[4,256]{1,0:T(4,128)S(1)} %maximum_bitcast_fusion), channel_id=1, source_target_pairs={{0,8},{4,12},{8,0},{12,4},{1,9},{5,13},{9,1},{13,5},{2,10},{6,14},... | collective-permute-start | bytes 12296 | tf_op jit(solution)/shard_map/ppermute | solution.py:42
  6.7 7.1 %collective-permute-start = (f32[4,256]{1,0:T(4,128)S(1)}, f32[4,256]{1,0:T(4,128)S(1)}, u32[]{:S(2)}, u32[]{:S(2)}) collective-permute-start(f32[4,256]{1,0:T(4,128)S(1)} %maximum_bitcast_fusion), channel_id=1, source_target_pairs={{0,4},{4,0},{8,12},{12,8},{1,5},{5,1},{9,13},{13,9},{2,6},{6,2},{1... | collective-permute-start | bytes 12296 | tf_op jit(solution)/shard_map/ppermute | solution.py:42
  10.3 25.6 %collective-permute-start.4 = (bf16[256,2048]{1,0:T(8,128)(2,1)S(1)}, bf16[256,2048]{1,0:T(8,128)(2,1)S(1)}, u32[]{:S(2)}, u32[]{:S(2)}) collective-permute-start(bf16[256,2048]{1,0:T(8,128)(2,1)S(1)} %fusion.53), channel_id=1, source_target_pairs={{0,8},{4,12},{8,0},{12,4},{1,9},{5,13},{9,1},{13,5},{2,10},{6,14},... | collective-permute-start | bytes 3145736 | tf_op jit(solution)/shard_map/ppermute | solution.py:42
  10.5 5.1 %collective-permute-start.1 = (bf16[256,2048]{1,0:T(8,128)(2,1)S(1)}, bf16[256,2048]{1,0:T(8,128)(2,1)}, u32[]{:S(2)}, u32[]{:S(2)}) collective-permute-start(bf16[256,2048]{1,0:T(8,128)(2,1)S(1)} %fusion.53), channel_id=1, source_target_pairs={{0,4},{4,0},{8,12},{12,8},{1,5},{5,1},{9,13},{13,9},{2,6},{6,2},{1... | collective-permute-start | bytes 3145736 | tf_op jit(solution)/shard_map/ppermute | solution.py:42
  14.1 1.2 %collective-permute-start.5 = (f32[4,256]{1,0:T(4,128)S(1)}, f32[4,256]{1,0:T(4,128)S(1)}, u32[]{:S(2)}, u32[]{:S(2)}) collective-permute-start(f32[4,256]{1,0:T(4,128)S(1)} %collective-permute-done.3), channel_id=1, source_target_pairs={{0,4},{4,0},{8,12},{12,8},{1,5},{5,1},{9,13},{13,9},{2,6},{6,2},{1... | collective-permute-start | bytes 12296 | tf_op jit(solution)/shard_map/ppermute | solution.py:42
  17.2 3.8 %copy-start.2 = (bf16[128,2048]{1,0:T(8,128)(2,1)S(1)}, bf16[128,2048]{1,0:T(8,128)(2,1)}, u32[]{:S(2)}) copy-start(bf16[128,2048]{1,0:T(8,128)(2,1)} %convolution_convert_fusion.11) | copy-start | bytes 1572868
  17.2 3.8 %copy-start.5 = (bf16[1,2048,1024]{2,1,0:T(8,128)(2,1)S(1)}, bf16[1,2048,1024]{2,1,0:T(8,128)(2,1)}, u32[]{:S(2)}) copy-start(bf16[1,2048,1024]{2,1,0:T(8,128)(2,1)} %param.16) | copy-start | bytes 12582916
  21.0 3.0 %copy-start.1 = (bf16[128,2048]{1,0:T(8,128)(2,1)S(1)}, bf16[128,2048]{1,0:T(8,128)(2,1)}, u32[]{:S(2)}) copy-start(bf16[128,2048]{1,0:T(8,128)(2,1)} %convolution_convert_fusion.9) | copy-start | bytes 1572868
  29.7 6.9 %copy-start.9 = (bf16[1,1024,2048]{2,1,0:T(8,128)(2,1)S(1)}, bf16[1,1024,2048]{2,1,0:T(8,128)(2,1)}, u32[]{:S(2)}) copy-start(bf16[1,1024,2048]{2,1,0:T(8,128)(2,1)} %param.21) | copy-start | bytes 12582916
  36.0 2.7 %collective-permute-start.6 = (bf16[256,2048]{1,0:T(8,128)(2,1)S(1)}, bf16[256,2048]{1,0:T(8,128)(2,1)S(1)}, u32[]{:S(2)}, u32[]{:S(2)}) collective-permute-start(bf16[256,2048]{1,0:T(8,128)(2,1)S(1)} %collective-permute-done.4), channel_id=1, source_target_pairs={{0,4},{4,0},{8,12},{12,8},{1,5},{5,1},{9,13},{13,9},{2,6},{6,2},{1... | collective-permute-start | bytes 3145736 | tf_op jit(solution)/shard_map/ppermute | solution.py:42
  47.9 2.4 %collective-permute-start.7 = (bf16[128,2048]{1,0:T(8,128)(2,1)S(1)}, bf16[128,2048]{1,0:T(8,128)(2,1)S(1)}, u32[]{:S(2)}, u32[]{:S(2)}) collective-permute-start(bf16[128,2048]{1,0:T(8,128)(2,1)S(1)} %convolution_convert_fusion.2), channel_id=1, source_target_pairs={{0,4},{4,0},{8,12},{12,8},{1,5},{5,1},{9,13},{13,9},{2,6},{6,2},{1... | collective-permute-start | bytes 1572872 | tf_op jit(solution)/shard_map/ppermute | solution.py:42
  48.7 5.2 %collective-permute-start.2 = (bf16[128,2048]{1,0:T(8,128)(2,1)S(1)}, bf16[128,2048]{1,0:T(8,128)(2,1)S(1)}, u32[]{:S(2)}, u32[]{:S(2)}) collective-permute-start(bf16[128,2048]{1,0:T(8,128)(2,1)S(1)} %convolution_convert_fusion.7), channel_id=1, source_target_pairs={{0,4},{4,0},{8,12},{12,8},{1,5},{5,1},{9,13},{13,9},{2,6},{6,2},{1... | collective-permute-start | bytes 1572872 | tf_op jit(solution)/shard_map/ppermute | solution.py:42
  49.2 18.5 %collective-permute-start.12 = (bf16[128,2048]{1,0:T(8,128)(2,1)S(1)}, bf16[128,2048]{1,0:T(8,128)(2,1)S(1)}, u32[]{:S(2)}, u32[]{:S(2)}) collective-permute-start(bf16[128,2048]{1,0:T(8,128)(2,1)S(1)} %convolution_convert_fusion.1), channel_id=1, source_target_pairs={{0,4},{4,0},{8,12},{12,8},{1,5},{5,1},{9,13},{13,9},{2,6},{6,2},{1... | collective-permute-start | bytes 1572872 | tf_op jit(solution)/shard_map/ppermute | solution.py:42
  50.0 2.1 %collective-permute-start.13 = (bf16[128,2048]{1,0:T(8,128)(2,1)S(1)}, bf16[128,2048]{1,0:T(8,128)(2,1)S(1)}, u32[]{:S(2)}, u32[]{:S(2)}) collective-permute-start(bf16[128,2048]{1,0:T(8,128)(2,1)S(1)} %convolution_convert_fusion), channel_id=1, source_target_pairs={{0,4},{4,0},{8,12},{12,8},{1,5},{5,1},{9,13},{13,9},{2,6},{6,2},{1... | collective-permute-start | bytes 1572872 | tf_op jit(solution)/shard_map/ppermute | solution.py:42
  50.6 14.8 %collective-permute-start.8 = (bf16[128,2048]{1,0:T(8,128)(2,1)S(1)}, bf16[128,2048]{1,0:T(8,128)(2,1)S(1)}, u32[]{:S(2)}, u32[]{:S(2)}) collective-permute-start(bf16[128,2048]{1,0:T(8,128)(2,1)S(1)} %add_convert_fusion.1), channel_id=1, source_target_pairs={{0,8},{4,12},{8,0},{12,4},{1,9},{5,13},{9,1},{13,5},{2,10},{6,14},... | collective-permute-start | bytes 1572872 | tf_op jit(solution)/shard_map/ppermute | solution.py:42
  52.5 23.6 %collective-permute-start.14 = (bf16[128,2048]{1,0:T(8,128)(2,1)S(1)}, bf16[128,2048]{1,0:T(8,128)(2,1)S(1)}, u32[]{:S(2)}, u32[]{:S(2)}) collective-permute-start(bf16[128,2048]{1,0:T(8,128)(2,1)S(1)} %add_convert_fusion), channel_id=1, source_target_pairs={{0,8},{4,12},{8,0},{12,4},{1,9},{5,13},{9,1},{13,5},{2,10},{6,14},... | collective-permute-start | bytes 1572872 | tf_op jit(solution)/shard_map/ppermute | solution.py:42
  65.7 23.0 %collective-permute-start.9 = (bf16[128,512]{1,0:T(8,128)(2,1)S(1)}, bf16[128,512]{1,0:T(8,128)(2,1)S(1)}, u32[]{:S(2)}, u32[]{:S(2)}) collective-permute-start(bf16[128,512]{1,0:T(8,128)(2,1)S(1)} %get-tuple-element.23), channel_id=1, source_target_pairs={{0,1},{1,0},{2,3},{3,2},{4,5},{5,4},{6,7},{7,6},{8,9},{9,8},{10,11... | collective-permute-start | bytes 393224 | tf_op jit(solution)/shard_map/ppermute | solution.py:42
  67.3 11.1 %collective-permute-start.10 = (bf16[128,512]{1,0:T(8,128)(2,1)S(1)}, bf16[128,512]{1,0:T(8,128)(2,1)S(1)}, u32[]{:S(2)}, u32[]{:S(2)}) collective-permute-start(bf16[128,512]{1,0:T(8,128)(2,1)S(1)} %get-tuple-element.24), channel_id=1, source_target_pairs={{0,1},{1,0},{2,3},{3,2},{4,5},{5,4},{6,7},{7,6},{8,9},{9,8},{10,11... | collective-permute-start | bytes 393224 | tf_op jit(solution)/shard_map/ppermute | solution.py:42
  76.3 12.4 %collective-permute-start.15 = (bf16[128,512]{1,0:T(8,128)(2,1)S(1)}, bf16[128,512]{1,0:T(8,128)(2,1)S(1)}, u32[]{:S(2)}, u32[]{:S(2)}) collective-permute-start(bf16[128,512]{1,0:T(8,128)(2,1)S(1)} %get-tuple-element.25), channel_id=1, source_target_pairs={{0,1},{1,0},{2,3},{3,2},{4,5},{5,4},{6,7},{7,6},{8,9},{9,8},{10,11... | collective-permute-start | bytes 393224 | tf_op jit(solution)/shard_map/ppermute | solution.py:42
  78.0 9.0 %collective-permute-start.16 = (bf16[128,512]{1,0:T(8,128)(2,1)S(1)}, bf16[128,512]{1,0:T(8,128)(2,1)S(1)}, u32[]{:S(2)}, u32[]{:S(2)}) collective-permute-start(bf16[128,512]{1,0:T(8,128)(2,1)S(1)} %get-tuple-element.26), channel_id=1, source_target_pairs={{0,1},{1,0},{2,3},{3,2},{4,5},{5,4},{6,7},{7,6},{8,9},{9,8},{10,11... | collective-permute-start | bytes 393224 | tf_op jit(solution)/shard_map/ppermute | solution.py:42
  78.5 10.2 %collective-permute-start.11 = (bf16[128,512]{1,0:T(8,128)(2,1)S(1)}, bf16[128,512]{1,0:T(8,128)(2,1)S(1)}, u32[]{:S(2)}, u32[]{:S(2)}) collective-permute-start(bf16[128,512]{1,0:T(8,128)(2,1)S(1)} %add_convert_fusion.3), channel_id=1, source_target_pairs={{0,2},{1,3},{2,0},{3,1},{4,6},{5,7},{6,4},{7,5},{8,10},{9,11},{10,... | collective-permute-start | bytes 393224 | tf_op jit(solution)/shard_map/ppermute | solution.py:42
  87.0 7.8 %collective-permute-start.17 = (bf16[128,512]{1,0:T(8,128)(2,1)S(1)}, bf16[128,512]{1,0:T(8,128)(2,1)S(1)}, u32[]{:S(2)}, u32[]{:S(2)}) collective-permute-start(bf16[128,512]{1,0:T(8,128)(2,1)S(1)} %add_convert_fusion.2), channel_id=1, source_target_pairs={{0,2},{1,3},{2,0},{3,1},{4,6},{5,7},{6,4},{7,5},{8,10},{9,11},{10,... | collective-permute-start | bytes 393224 | tf_op jit(solution)/shard_map/ppermute | solution.py:42
  (4 other events, 9.7 us)

commit v4 on v3

--- a/solution.py
+++ b/solution.py
@@ -2,9 +2,6 @@
 import jax.numpy as jnp
 from jax import lax
 from jax.sharding import PartitionSpec as P
-
-
-CHUNKS = 2
 
 
 def dot32(a, b):
@@ -51,13 +48,15 @@
     return blocks
 
 
-def reduce_near(blocks, axis):
-    bit, count = 1, lax.axis_size(axis)
-    while bit < count:
+def bits_of(axis):
+    return [1 << k for k in range(lax.axis_size(axis).bit_length() - 1)]
+
+
+def reduce_near(blocks, axis, bits):
+    for bit in bits:
         sent = {r: swap(v.astype(jnp.bfloat16), axis, bit) for r, v in blocks.items() if r & bit}
         blocks = {r: v + sent[r | bit].astype(jnp.float32) for r, v in blocks.items() if not r & bit}
-        bit *= 2
-    return blocks[0]
+    return blocks
 
 
 def by_tokens(modded, targets, weights, capacity, experts, shards, sets):
@@ -92,24 +91,32 @@
             for at, r in enumerate(group):
                 served[r].append(out[at * capacity : (at + 1) * capacity])
     served = {r: jnp.concatenate(v, axis=0) for r, v in served.items()}
+    def columns_of(term):
+        split = {
+            r: lax.dynamic_slice_in_dim(term, (mine ^ r) * columns, columns, 1)
+            for r in range(shards)
+        }
+        return reduce_near(split, "tensor", bits_of("tensor"))[0]
+
+    close, far = bits_of("expert")[:1], bits_of("expert")[1:]
+    cut = rows * 5 // 8 // 16 * 16
     sums = []
-    step = rows // CHUNKS
-    for c in range(CHUNKS):
+    for lower, upper in ((0, cut), (cut, rows)):
         terms = {
             r: lax.dot_general(
-                pick[r][:, c * step : (c + 1) * step],
+                pick[r][:, lower:upper],
                 served[r],
                 (((0,), (0,)), ((), ())),
                 preferred_element_type=jnp.float32,
             )
             for r in order
         }
-        own = reduce_near(terms, "expert")
-        split = {
-            r: lax.dynamic_slice_in_dim(own, (mine ^ r) * columns, columns, 1)
-            for r in range(shards)
-        }
-        sums.append(reduce_near(split, "tensor"))
+        chip = reduce_near(terms, "expert", close)
+        if lower == 0:
+            sums.append(columns_of(reduce_near(chip, "expert", far)[0]))
+        else:
+            narrow = {r: columns_of(v) for r, v in chip.items()}
+            sums.append(reduce_near(narrow, "expert", far)[0])
     return jnp.concatenate(sums, axis=0)
 
 

time: 96.1 us -> 85.8 us (0.89)
  waiting for transfers between devices: 40.2 us -> 22.4 us
  starting transfers between devices: 15.2 us -> 20.9 us
  local copies, waits for them, and re-layouts: 2.33 us -> 3.97 us
    ppermute x18 -> x21, waiting for transfers between devices: 40.2 us -> 22.4 us  [swap(): return lax.ppermute(value, axis, [(i, i ^ bit) for i in range(count)])]
    ppermute x18 -> x21, starting transfers between devices: 15.2 us -> 20.9 us  [swap(): return lax.ppermute(value, axis, [(i, i ^ bit) for i in range(count)])]
    unnamed x20, local copies, waits for them, and re-layouts: 1.82 us -> 3.4 us
  transfers between devices with their start and end apart: 18 -> 21, of which waited for: 8 -> 7; matrix products, arithmetic and copies ran while one was open for 25% -> 39% of each run, Pallas kernels for 0% -> 0%
where the time goes in v4:
time: 85.8 us; the launch traced here: 85.3 us
  matrix products  28.1 us (33%)
  waiting for transfers between devices  22.4 us (26%)
  starting transfers between devices  20.9 us (24%)
  other arithmetic  9.39 us (11%)
  local copies, waits for them, and re-layouts  3.97 us (5%)
    dot_general x21, matrix products, dot32(): return jnp.dot(a, b, preferred_element_type=jnp.float32)  24.8 us
    ppermute x21, waiting for transfers between devices, swap(): return lax.ppermute(value, axis, [(i, i ^ bit) for i in range(count)])  22.4 us
    ppermute x21, starting transfers between devices, swap(): return lax.ppermute(value, axis, [(i, i ^ bit) for i in range(count)])  20.9 us
    unnamed x20, local copies, waits for them, and re-layouts  3.4 us
    dot_general x8, matrix products, by_tokens(): lax.dot_general(pick[r][:, lower:upper], served[r], (((0,), (0,)), ((), (...  3.27 us
  transfers between devices with their start and end apart: 21, of which 7 were waited for; matrix products, arithmetic and copies ran while one was open for 39% of the time, Pallas kernels for 0%

profile of v4, /device:TPU:0, one launch (start us, length us, event | category | flops | bytes accessed | tf_op | source)
XLA Modules:
  0.0 85.3 jit_solution(12764409337332546771)
XLA Ops:
  3.8 2.9 %collective-permute-start.3 = (f32[4,256]{1,0:T(4,128)S(1)}, f32[4,256]{1,0:T(4,128)S(1)}, u32[]{:S(2)}, u32[]{:S(2)}) collective-permute-start(f32[4,256]{1,0:T(4,128)S(1)} %maximum_bitcast_fusion), channel_id=1, source_target_pairs={{0,8},{4,12},{8,0},{12,4},{1,9},{5,13},{9,1},{13,5},{2,10},{6,14},... | collective-permute-start | bytes 12296 | tf_op jit(solution)/shard_map/ppermute | solution.py:39
  6.7 1.4 %convert_reduce_fusion = f32[256]{0:T(256)S(1)} fusion(bf16[256,2048]{1,0:T(8,128)(2,1)} %param.11), kind=kLoop, calls=%fused_computation.29 | loop fusion | flops 1048320 | bytes 1049600 | tf_op jit(solution)/shard_map/reduce_sum | solution.py:25
  8.2 1.6 %fusion.50 = f32[256]{0:T(256)S(1)} fusion(bf16[256,2048]{1,0:T(8,128)(2,1)} %param.11, f32[256]{0:T(256)S(1)} %broadcast_multiply_fusion), kind=kLoop, calls=%fused_computation.48 | loop fusion | flops 2096896 | bytes 1050624 | tf_op jit(solution)/shard_map/reduce_sum | solution.py:27
  15.6 1.5 %convolution_convert_fusion.8 = bf16[128,2048]{1,0:T(8,128)(2,1)S(1)} fusion(bf16[256,2048]{1,0:T(8,128)(2,1)} %collective-permute-done.1, pred[256,256]{1,0:T(32,128)(4,1)S(1)} %fusion.66), kind=kOutput, calls=%fused_computation.44 | convolution fusion | flops 134479872 | bytes 1605632 | tf_op jit(solution)/shard_map/dot_general | solution.py:8
  17.2 3.7 %fusion.18 = f32[256,1024]{1,0:T(8,128)S(1)} fusion(bf16[1,2048,1024]{2,1,0:T(8,128)(2,1)} %param.17, bf16[128,2048]{1,0:T(8,128)(2,1)S(1)} %convolution_convert_fusion.8, bf16[128,2048]{1,0:T(8,128)(2,1)} %convolution_convert_fusion.9), kind=kOutput, calls=%fused_computation.18 | convolution fusion | flops 1075838976 | bytes 6291456 | tf_op jit(solution)/shard_map/dot_general | solution.py:8
  22.3 1.7 %convolution_convert_fusion.6 = bf16[128,2048]{1,0:T(8,128)(2,1)S(1)} fusion(bf16[256,2048]{1,0:T(8,128)(2,1)} %collective-permute-done.1, pred[256,256]{1,0:T(32,128)(4,1)S(1)} %fusion.66), kind=kOutput, calls=%fused_computation.42 | convolution fusion | flops 134479872 | bytes 1605632 | tf_op jit(solution)/shard_map/dot_general | solution.py:8
  26.1 1.3 %fusion.45 = bf16[256,2048]{1,0:T(8,128)(2,1)S(1)} fusion(bf16[1,1024,2048]{2,1,0:T(8,128)(2,1)S(1)} %copy-done.8, f32[256]{0:T(256)S(1)} %bitcast.128, f32[256,1024]{1,0:T(8,128)S(1)} %fusion.18, f32[256,1024]{1,0:T(8,128)S(1)} %fusion.22), kind=kOutput, calls=%fused_computation.33 | convolution fusion | flops 1076363264 | bytes 7341056 | tf_op jit(solution)/shard_map/dot_general | solution.py:8
  30.5 1.3 %fusion.39 = bf16[256,2048]{1,0:T(8,128)(2,1)S(1)} fusion(bf16[1,1024,2048]{2,1,0:T(8,128)(2,1)S(1)} %copy-done.9, f32[256]{0:T(256)S(1)} %bitcast.127, f32[256,1024]{1,0:T(8,128)S(1)} %fusion.6, f32[256,1024]{1,0:T(8,128)S(1)} %fusion.10), kind=kOutput, calls=%fused_computation.31 | convolution fusion | flops 1076363264 | bytes 7341056 | tf_op jit(solution)/shard_map/dot_general | solution.py:8
  31.8 4.1 %collective-permute-done.4 = bf16[256,2048]{1,0:T(8,128)(2,1)S(1)} collective-permute-done((bf16[256,2048]{1,0:T(8,128)(2,1)S(1)}, bf16[256,2048]{1,0:T(8,128)(2,1)S(1)}, u32[]{:S(2)}, u32[]{:S(2)}) %collective-permute-start.4) | collective-permute-done | bytes 1048608 | tf_op jit(solution)/shard_map/ppermute | solution.py:39
  39.7 1.5 %fusion.16 = f32[256,1024]{1,0:T(8,128)S(1)} fusion(bf16[1,2048,1024]{2,1,0:T(8,128)(2,1)S(1)} %copy-done.4, bf16[128,2048]{1,0:T(8,128)(2,1)S(1)} %convolution_convert_fusion.4, bf16[128,2048]{1,0:T(8,128)(2,1)S(1)} %convolution_convert_fusion.5), kind=kOutput, calls=%fused_computation.16 | convolution fusion | flops 1075838976 | bytes 6291456 | tf_op jit(solution)/shard_map/dot_general | solution.py:8
  41.1 1.3 %fusion.20 = f32[256,1024]{1,0:T(8,128)S(1)} fusion(bf16[1,2048,1024]{2,1,0:T(8,128)(2,1)S(1)} %copy-done.5, bf16[128,2048]{1,0:T(8,128)(2,1)S(1)} %convolution_convert_fusion.4, bf16[128,2048]{1,0:T(8,128)(2,1)S(1)} %convolution_convert_fusion.5), kind=kOutput, calls=%fused_computation.20 | convolution fusion | flops 1075838976 | bytes 6291456 | tf_op jit(solution)/shard_map/dot_general | solution.py:8
  44.0 1.3 %fusion.8 = f32[256,1024]{1,0:T(8,128)S(1)} fusion(bf16[1,2048,1024]{2,1,0:T(8,128)(2,1)S(1)} %copy-done.7, bf16[128,2048]{1,0:T(8,128)(2,1)S(1)} %convolution_convert_fusion.2, bf16[128,2048]{1,0:T(8,128)(2,1)S(1)} %convolution_convert_fusion.3), kind=kOutput, calls=%fused_computation.8 | convolution fusion | flops 1075838976 | bytes 6291456 | tf_op jit(solution)/shard_map/dot_general | solution.py:8
  45.3 1.3 %fusion.42 = bf16[256,2048]{1,0:T(8,128)(2,1)S(1)} fusion(bf16[1,1024,2048]{2,1,0:T(8,128)(2,1)S(1)} %copy-done.8, f32[256]{0:T(256)S(1)} %bitcast.126, f32[256,1024]{1,0:T(8,128)S(1)} %fusion.16, f32[256,1024]{1,0:T(8,128)S(1)} %fusion.20), kind=kOutput, calls=%fused_computation.32 | convolution fusion | flops 1076363264 | bytes 7341056 | tf_op jit(solution)/shard_map/dot_general | solution.py:8
  46.7 1.3 %fusion.36 = bf16[256,2048]{1,0:T(8,128)(2,1)S(1)} fusion(bf16[1,1024,2048]{2,1,0:T(8,128)(2,1)S(1)} %copy-done.9, f32[256]{0:T(256)S(1)} %bitcast.125, f32[256,1024]{1,0:T(8,128)S(1)} %fusion.4, f32[256,1024]{1,0:T(8,128)S(1)} %fusion.8), kind=kOutput, calls=%fused_computation.30 | convolution fusion | flops 1076363264 | bytes 7341056 | tf_op jit(solution)/shard_map/dot_general | solution.py:8
  50.5 1.6 %collective-permute-start.13 = (bf16[96,512]{1,0:T(8,128)(2,1)S(1)}, bf16[96,512]{1,0:T(8,128)(2,1)S(1)}, u32[]{:S(2)}, u32[]{:S(2)}) collective-permute-start(bf16[96,512]{1,0:T(8,128)(2,1)S(1)} %get-tuple-element.33), channel_id=1, source_target_pairs={{0,1},{1,0},{2,3},{3,2},{4,5},{5,4},{6,7},{7,6},{8,9},{9,8},{10,11... | collective-permute-start | bytes 294920 | tf_op jit(solution)/shard_map/ppermute | solution.py:39
  53.8 1.9 %collective-permute-start.18 = (bf16[96,512]{1,0:T(8,128)(2,1)S(1)}, bf16[96,512]{1,0:T(8,128)(2,1)S(1)}, u32[]{:S(2)}, u32[]{:S(2)}) collective-permute-start(bf16[96,512]{1,0:T(8,128)(2,1)S(1)} %get-tuple-element.36), channel_id=1, source_target_pairs={{0,1},{1,0},{2,3},{3,2},{4,5},{5,4},{6,7},{7,6},{8,9},{9,8},{10,11... | collective-permute-start | bytes 294920 | tf_op jit(solution)/shard_map/ppermute | solution.py:39
  55.7 2.5 %collective-permute-done.14 = bf16[96,512]{1,0:T(8,128)(2,1)S(1)} collective-permute-done((bf16[96,512]{1,0:T(8,128)(2,1)S(1)}, bf16[96,512]{1,0:T(8,128)(2,1)S(1)}, u32[]{:S(2)}, u32[]{:S(2)}) %collective-permute-start.14) | collective-permute-done | bytes 98336 | tf_op jit(solution)/shard_map/ppermute | solution.py:39
  58.2 2.7 %collective-permute-start.15 = (bf16[96,512]{1,0:T(8,128)(2,1)S(1)}, bf16[96,512]{1,0:T(8,128)(2,1)S(1)}, u32[]{:S(2)}, u32[]{:S(2)}) collective-permute-start(bf16[96,512]{1,0:T(8,128)(2,1)S(1)} %add_convert_fusion.4), channel_id=1, source_target_pairs={{0,2},{1,3},{2,0},{3,1},{4,6},{5,7},{6,4},{7,5},{8,10},{9,11},{10,... | collective-permute-start | bytes 294920 | tf_op jit(solution)/shard_map/ppermute | solution.py:39
  60.8 1.7 %collective-permute-start.17 = (bf16[96,512]{1,0:T(8,128)(2,1)S(1)}, bf16[96,512]{1,0:T(8,128)(2,1)S(1)}, u32[]{:S(2)}, u32[]{:S(2)}) collective-permute-start(bf16[96,512]{1,0:T(8,128)(2,1)S(1)} %get-tuple-element.35), channel_id=1, source_target_pairs={{0,1},{1,0},{2,3},{3,2},{4,5},{5,4},{6,7},{7,6},{8,9},{9,8},{10,11... | collective-permute-start | bytes 294920 | tf_op jit(solution)/shard_map/ppermute | solution.py:39
  63.7 5.4 %collective-permute-done.8 = bf16[160,2048]{1,0:T(8,128)(2,1)S(1)} collective-permute-done((bf16[160,2048]{1,0:T(8,128)(2,1)S(1)}, bf16[160,2048]{1,0:T(8,128)(2,1)S(1)}, u32[]{:S(2)}, u32[]{:S(2)}) %collective-permute-start.8) | collective-permute-done | bytes 655392 | tf_op jit(solution)/shard_map/ppermute | solution.py:39
  69.5 1.6 %collective-permute-start.10 = (bf16[160,512]{1,0:T(8,128)(2,1)S(1)}, bf16[160,512]{1,0:T(8,128)(2,1)S(1)}, u32[]{:S(2)}, u32[]{:S(2)}) collective-permute-start(bf16[160,512]{1,0:T(8,128)(2,1)S(1)} %get-tuple-element.24), channel_id=1, source_target_pairs={{0,1},{1,0},{2,3},{3,2},{4,5},{5,4},{6,7},{7,6},{8,9},{9,8},{10,11... | collective-permute-start | bytes 491528 | tf_op jit(solution)/shard_map/ppermute | solution.py:39
  72.1 3.8 %collective-permute-done.10 = bf16[160,512]{1,0:T(8,128)(2,1)S(1)} collective-permute-done((bf16[160,512]{1,0:T(8,128)(2,1)S(1)}, bf16[160,512]{1,0:T(8,128)(2,1)S(1)}, u32[]{:S(2)}, u32[]{:S(2)}) %collective-permute-start.10) | collective-permute-done | bytes 163872 | tf_op jit(solution)/shard_map/ppermute | solution.py:39
  76.0 3.4 %collective-permute-start.11 = (bf16[160,512]{1,0:T(8,128)(2,1)S(1)}, bf16[160,512]{1,0:T(8,128)(2,1)S(1)}, u32[]{:S(2)}, u32[]{:S(2)}) collective-permute-start(bf16[160,512]{1,0:T(8,128)(2,1)S(1)} %add_convert_fusion.1), channel_id=1, source_target_pairs={{0,2},{1,3},{2,0},{3,1},{4,6},{5,7},{6,4},{7,5},{8,10},{9,11},{10,... | collective-permute-start | bytes 491528 | tf_op jit(solution)/shard_map/ppermute | solution.py:39
  79.4 5.0 %collective-permute-done.11 = bf16[160,512]{1,0:T(8,128)(2,1)S(1)} collective-permute-done((bf16[160,512]{1,0:T(8,128)(2,1)S(1)}, bf16[160,512]{1,0:T(8,128)(2,1)S(1)}, u32[]{:S(2)}, u32[]{:S(2)}) %collective-permute-start.11) | collective-permute-done | bytes 163872 | tf_op jit(solution)/shard_map/ppermute | solution.py:39
  (126 shorter events, 28.8 us)
Async XLA Ops:
  0.0 9.9 %copy-start = (bf16[256,2048]{1,0:T(8,128)(2,1)S(1)}, bf16[256,2048]{1,0:T(8,128)(2,1)}, u32[]{:S(2)}) copy-start(bf16[256,2048]{1,0:T(8,128)(2,1)} %param.11) | copy-start | bytes 3145732
  0.0 9.8 %copy-start.3 = (f32[1,6144]{1,0:T(1,128)S(1)}, f32[1,6144]{1,0:T(1,128)}, u32[]{:S(2)}) copy-start(f32[1,6144]{1,0:T(1,128)} %param.14) | copy-start | bytes 73732
  3.8 9.8 %collective-permute-start.3 = (f32[4,256]{1,0:T(4,128)S(1)}, f32[4,256]{1,0:T(4,128)S(1)}, u32[]{:S(2)}, u32[]{:S(2)}) collective-permute-start(f32[4,256]{1,0:T(4,128)S(1)} %maximum_bitcast_fusion), channel_id=1, source_target_pairs={{0,8},{4,12},{8,0},{12,4},{1,9},{5,13},{9,1},{13,5},{2,10},{6,14},... | collective-permute-start | bytes 12296 | tf_op jit(solution)/shard_map/ppermute | solution.py:39
  6.7 7.1 %collective-permute-start = (f32[4,256]{1,0:T(4,128)S(1)}, f32[4,256]{1,0:T(4,128)S(1)}, u32[]{:S(2)}, u32[]{:S(2)}) collective-permute-start(f32[4,256]{1,0:T(4,128)S(1)} %maximum_bitcast_fusion), channel_id=1, source_target_pairs={{0,4},{4,0},{8,12},{12,8},{1,5},{5,1},{9,13},{13,9},{2,6},{6,2},{1... | collective-permute-start | bytes 12296 | tf_op jit(solution)/shard_map/ppermute | solution.py:39
  10.3 25.6 %collective-permute-start.4 = (bf16[256,2048]{1,0:T(8,128)(2,1)S(1)}, bf16[256,2048]{1,0:T(8,128)(2,1)S(1)}, u32[]{:S(2)}, u32[]{:S(2)}) collective-permute-start(bf16[256,2048]{1,0:T(8,128)(2,1)S(1)} %fusion.53), channel_id=1, source_target_pairs={{0,8},{4,12},{8,0},{12,4},{1,9},{5,13},{9,1},{13,5},{2,10},{6,14},... | collective-permute-start | bytes 3145736 | tf_op jit(solution)/shard_map/ppermute | solution.py:39
  10.5 5.1 %collective-permute-start.1 = (bf16[256,2048]{1,0:T(8,128)(2,1)S(1)}, bf16[256,2048]{1,0:T(8,128)(2,1)}, u32[]{:S(2)}, u32[]{:S(2)}) collective-permute-start(bf16[256,2048]{1,0:T(8,128)(2,1)S(1)} %fusion.53), channel_id=1, source_target_pairs={{0,4},{4,0},{8,12},{12,8},{1,5},{5,1},{9,13},{13,9},{2,6},{6,2},{1... | collective-permute-start | bytes 3145736 | tf_op jit(solution)/shard_map/ppermute | solution.py:39
  14.1 1.2 %collective-permute-start.5 = (f32[4,256]{1,0:T(4,128)S(1)}, f32[4,256]{1,0:T(4,128)S(1)}, u32[]{:S(2)}, u32[]{:S(2)}) collective-permute-start(f32[4,256]{1,0:T(4,128)S(1)} %collective-permute-done.3), channel_id=1, source_target_pairs={{0,4},{4,0},{8,12},{12,8},{1,5},{5,1},{9,13},{13,9},{2,6},{6,2},{1... | collective-permute-start | bytes 12296 | tf_op jit(solution)/shard_map/ppermute | solution.py:39
  17.2 3.8 %copy-start.2 = (bf16[128,2048]{1,0:T(8,128)(2,1)S(1)}, bf16[128,2048]{1,0:T(8,128)(2,1)}, u32[]{:S(2)}) copy-start(bf16[128,2048]{1,0:T(8,128)(2,1)} %convolution_convert_fusion.9) | copy-start | bytes 1572868
  36.0 2.7 %collective-permute-start.6 = (bf16[256,2048]{1,0:T(8,128)(2,1)S(1)}, bf16[256,2048]{1,0:T(8,128)(2,1)S(1)}, u32[]{:S(2)}, u32[]{:S(2)}) collective-permute-start(bf16[256,2048]{1,0:T(8,128)(2,1)S(1)} %collective-permute-done.4), channel_id=1, source_target_pairs={{0,4},{4,0},{8,12},{12,8},{1,5},{5,1},{9,13},{13,9},{2,6},{6,2},{1... | collective-permute-start | bytes 3145736 | tf_op jit(solution)/shard_map/ppermute | solution.py:39
  36.5 13.5 %collective-permute-start.12 = (bf16[96,2048]{1,0:T(8,128)(2,1)S(1)}, bf16[96,2048]{1,0:T(8,128)(2,1)S(1)}, u32[]{:S(2)}, u32[]{:S(2)}) collective-permute-start(bf16[96,2048]{1,0:T(8,128)(2,1)S(1)} %convolution_convert_fusion.11), channel_id=1, source_target_pairs={{0,4},{4,0},{8,12},{12,8},{1,5},{5,1},{9,13},{13,9},{2,6},{6,2},{1... | collective-permute-start | bytes 1179656 | tf_op jit(solution)/shard_map/ppermute | solution.py:39
  37.5 25.1 %collective-permute-start.2 = (bf16[160,2048]{1,0:T(8,128)(2,1)S(1)}, bf16[160,2048]{1,0:T(8,128)(2,1)S(1)}, u32[]{:S(2)}, u32[]{:S(2)}) collective-permute-start(bf16[160,2048]{1,0:T(8,128)(2,1)S(1)} %convolution_convert_fusion.1), channel_id=1, source_target_pairs={{0,4},{4,0},{8,12},{12,8},{1,5},{5,1},{9,13},{13,9},{2,6},{6,2},{1... | collective-permute-start | bytes 1966088 | tf_op jit(solution)/shard_map/ppermute | solution.py:39
  48.5 4.0 %collective-permute-start.7 = (bf16[160,2048]{1,0:T(8,128)(2,1)S(1)}, bf16[160,2048]{1,0:T(8,128)(2,1)S(1)}, u32[]{:S(2)}, u32[]{:S(2)}) collective-permute-start(bf16[160,2048]{1,0:T(8,128)(2,1)S(1)} %convolution_convert_fusion), channel_id=1, source_target_pairs={{0,4},{4,0},{8,12},{12,8},{1,5},{5,1},{9,13},{13,9},{2,6},{6,2},{1... | collective-permute-start | bytes 1966088 | tf_op jit(solution)/shard_map/ppermute | solution.py:39
  49.4 3.9 %collective-permute-start.16 = (bf16[96,2048]{1,0:T(8,128)(2,1)S(1)}, bf16[96,2048]{1,0:T(8,128)(2,1)S(1)}, u32[]{:S(2)}, u32[]{:S(2)}) collective-permute-start(bf16[96,2048]{1,0:T(8,128)(2,1)S(1)} %convolution_convert_fusion.10), channel_id=1, source_target_pairs={{0,4},{4,0},{8,12},{12,8},{1,5},{5,1},{9,13},{13,9},{2,6},{6,2},{1... | collective-permute-start | bytes 1179656 | tf_op jit(solution)/shard_map/ppermute | solution.py:39
  50.5 28.9 %collective-permute-start.13 = (bf16[96,512]{1,0:T(8,128)(2,1)S(1)}, bf16[96,512]{1,0:T(8,128)(2,1)S(1)}, u32[]{:S(2)}, u32[]{:S(2)}) collective-permute-start(bf16[96,512]{1,0:T(8,128)(2,1)S(1)} %get-tuple-element.33), channel_id=1, source_target_pairs={{0,1},{1,0},{2,3},{3,2},{4,5},{5,4},{6,7},{7,6},{8,9},{9,8},{10,11... | collective-permute-start | bytes 294920 | tf_op jit(solution)/shard_map/ppermute | solution.py:39
  52.1 6.1 %collective-permute-start.14 = (bf16[96,512]{1,0:T(8,128)(2,1)S(1)}, bf16[96,512]{1,0:T(8,128)(2,1)S(1)}, u32[]{:S(2)}, u32[]{:S(2)}) collective-permute-start(bf16[96,512]{1,0:T(8,128)(2,1)S(1)} %get-tuple-element.34), channel_id=1, source_target_pairs={{0,1},{1,0},{2,3},{3,2},{4,5},{5,4},{6,7},{7,6},{8,9},{9,8},{10,11... | collective-permute-start | bytes 294920 | tf_op jit(solution)/shard_map/ppermute | solution.py:39
  52.9 16.2 %collective-permute-start.8 = (bf16[160,2048]{1,0:T(8,128)(2,1)S(1)}, bf16[160,2048]{1,0:T(8,128)(2,1)S(1)}, u32[]{:S(2)}, u32[]{:S(2)}) collective-permute-start(bf16[160,2048]{1,0:T(8,128)(2,1)S(1)} %add_convert_fusion), channel_id=1, source_target_pairs={{0,8},{4,12},{8,0},{12,4},{1,9},{5,13},{9,1},{13,5},{2,10},{6,14},... | collective-permute-start | bytes 1966088 | tf_op jit(solution)/shard_map/ppermute | solution.py:39
  53.8 7.1 %collective-permute-start.18 = (bf16[96,512]{1,0:T(8,128)(2,1)S(1)}, bf16[96,512]{1,0:T(8,128)(2,1)S(1)}, u32[]{:S(2)}, u32[]{:S(2)}) collective-permute-start(bf16[96,512]{1,0:T(8,128)(2,1)S(1)} %get-tuple-element.36), channel_id=1, source_target_pairs={{0,1},{1,0},{2,3},{3,2},{4,5},{5,4},{6,7},{7,6},{8,9},{9,8},{10,11... | collective-permute-start | bytes 294920 | tf_op jit(solution)/shard_map/ppermute | solution.py:39
  58.2 21.2 %collective-permute-start.15 = (bf16[96,512]{1,0:T(8,128)(2,1)S(1)}, bf16[96,512]{1,0:T(8,128)(2,1)S(1)}, u32[]{:S(2)}, u32[]{:S(2)}) collective-permute-start(bf16[96,512]{1,0:T(8,128)(2,1)S(1)} %add_convert_fusion.4), channel_id=1, source_target_pairs={{0,2},{1,3},{2,0},{3,1},{4,6},{5,7},{6,4},{7,5},{8,10},{9,11},{10,... | collective-permute-start | bytes 294920 | tf_op jit(solution)/shard_map/ppermute | solution.py:39
  60.8 10.3 %collective-permute-start.17 = (bf16[96,512]{1,0:T(8,128)(2,1)S(1)}, bf16[96,512]{1,0:T(8,128)(2,1)S(1)}, u32[]{:S(2)}, u32[]{:S(2)}) collective-permute-start(bf16[96,512]{1,0:T(8,128)(2,1)S(1)} %get-tuple-element.35), channel_id=1, source_target_pairs={{0,1},{1,0},{2,3},{3,2},{4,5},{5,4},{6,7},{7,6},{8,9},{9,8},{10,11... | collective-permute-start | bytes 294920 | tf_op jit(solution)/shard_map/ppermute | solution.py:39
  62.6 8.5 %collective-permute-start.19 = (bf16[96,512]{1,0:T(8,128)(2,1)S(1)}, bf16[96,512]{1,0:T(8,128)(2,1)S(1)}, u32[]{:S(2)}, u32[]{:S(2)}) collective-permute-start(bf16[96,512]{1,0:T(8,128)(2,1)S(1)} %add_convert_fusion.3), channel_id=1, source_target_pairs={{0,2},{1,3},{2,0},{3,1},{4,6},{5,7},{6,4},{7,5},{8,10},{9,11},{10,... | collective-permute-start | bytes 294920 | tf_op jit(solution)/shard_map/ppermute | solution.py:39
  69.5 6.5 %collective-permute-start.10 = (bf16[160,512]{1,0:T(8,128)(2,1)S(1)}, bf16[160,512]{1,0:T(8,128)(2,1)S(1)}, u32[]{:S(2)}, u32[]{:S(2)}) collective-permute-start(bf16[160,512]{1,0:T(8,128)(2,1)S(1)} %get-tuple-element.24), channel_id=1, source_target_pairs={{0,1},{1,0},{2,3},{3,2},{4,5},{5,4},{6,7},{7,6},{8,9},{9,8},{10,11... | collective-permute-start | bytes 491528 | tf_op jit(solution)/shard_map/ppermute | solution.py:39
  71.1 8.2 %collective-permute-start.20 = (bf16[96,512]{1,0:T(8,128)(2,1)S(1)}, bf16[96,512]{1,0:T(8,128)(2,1)S(1)}, u32[]{:S(2)}, u32[]{:S(2)}) collective-permute-start(bf16[96,512]{1,0:T(8,128)(2,1)S(1)} %add_convert_fusion.2), channel_id=1, source_target_pairs={{0,8},{4,12},{8,0},{12,4},{1,9},{5,13},{9,1},{13,5},{2,10},{6,14},... | collective-permute-start | bytes 294920 | tf_op jit(solution)/shard_map/ppermute | solution.py:39
  71.8 7.7 %collective-permute-start.9 = (bf16[160,512]{1,0:T(8,128)(2,1)S(1)}, bf16[160,512]{1,0:T(8,128)(2,1)S(1)}, u32[]{:S(2)}, u32[]{:S(2)}) collective-permute-start(bf16[160,512]{1,0:T(8,128)(2,1)S(1)} %get-tuple-element.23), channel_id=1, source_target_pairs={{0,1},{1,0},{2,3},{3,2},{4,5},{5,4},{6,7},{7,6},{8,9},{9,8},{10,11... | collective-permute-start | bytes 491528 | tf_op jit(solution)/shard_map/ppermute | solution.py:39
  76.0 8.4 %collective-permute-start.11 = (bf16[160,512]{1,0:T(8,128)(2,1)S(1)}, bf16[160,512]{1,0:T(8,128)(2,1)S(1)}, u32[]{:S(2)}, u32[]{:S(2)}) collective-permute-start(bf16[160,512]{1,0:T(8,128)(2,1)S(1)} %add_convert_fusion.1), channel_id=1, source_target_pairs={{0,2},{1,3},{2,0},{3,1},{4,6},{5,7},{6,4},{7,5},{8,10},{9,11},{10,... | collective-permute-start | bytes 491528 | tf_op jit(solution)/shard_map/ppermute | solution.py:39
  (7 other events, 18.5 us)

commit v5 on v4

--- a/solution.py
+++ b/solution.py
@@ -9,16 +9,20 @@
 
 
 def pair_targets(ids, partner, experts, capacity):
-    rows = ids.shape[0]
-    onehot = (ids[:, :, None] == jnp.arange(experts, dtype=jnp.int32)).astype(jnp.float32)
-    named = (onehot[:, 0] + onehot[:, 1]).astype(jnp.bfloat16)
+    rows = ids.shape[1]
+    names = jnp.arange(experts, dtype=jnp.int32)[:, None]
+    onehot = [(ids[j][None, :] == names).astype(jnp.float32) for j in range(2)]
     order = jnp.arange(rows, dtype=jnp.int32)
-    before = (order[:, None] > order[None, :]).astype(jnp.bfloat16)
-    earlier = dot32(before, named)
-    ranks = jnp.sum(onehot * earlier[:, None, :], axis=2).astype(jnp.int32)
-    spare_of = jnp.sum(onehot * partner.astype(jnp.float32), axis=2).astype(jnp.int32)
-    server = jnp.where(ranks >= capacity, spare_of, ids)
-    return server * (2 * capacity) + ranks
+    before = (order[:, None] < order[None, :]).astype(jnp.bfloat16)
+    earlier = dot32((onehot[0] + onehot[1]).astype(jnp.bfloat16), before)
+    spares = partner.astype(jnp.float32)[:, None]
+    targets = []
+    for j in range(2):
+        rank = jnp.sum(onehot[j] * earlier, axis=0).astype(jnp.int32)
+        spare_of = jnp.sum(onehot[j] * spares, axis=0).astype(jnp.int32)
+        server = jnp.where(rank >= capacity, spare_of, ids[j])
+        targets.append(server * (2 * capacity) + rank)
+    return jnp.stack(targets)
 
 
 def modulate(values, mod_row, width):
@@ -65,7 +69,7 @@
     slots = 2 * capacity
     me = lax.axis_index("expert")
     mine = lax.axis_index("tensor")
-    packed = jnp.concatenate((targets.astype(jnp.float32), weights), axis=1).T
+    packed = jnp.concatenate((targets.astype(jnp.float32), weights.T), axis=0)
     routes = gather_near(packed, "expert")
     seen = gather_near(modded, "expert")
     number = jnp.arange(slots, dtype=jnp.int32)[:, None]
@@ -125,7 +129,7 @@
     columns = width // shards
     slots = experts * 2 * capacity
     number = jnp.arange(slots, dtype=jnp.int32)
-    hits = [targets[:, j][:, None] == number[None, :] for j in range(2)]
+    hits = [targets[j][:, None] == number[None, :] for j in range(2)]
     pick = (hits[0] | hits[1]).astype(jnp.bfloat16)
     outgoing = lax.dot_general(
         pick, modded, (((0,), (0,)), ((), ())), preferred_element_type=jnp.float32
@@ -174,7 +178,7 @@
     mod_row = modulation[0]
     tensor_start = lax.axis_index("tensor") * columns
     modded = modulate(tokens.astype(jnp.float32), mod_row, width)
-    targets = pair_targets(route_ids, partner, experts, capacity)
+    targets = pair_targets(route_ids.T, partner, experts, capacity)
     sets = ((w_gate[0], w_up[0], w_down[0]), (spare_gate[0], spare_up[0], spare_down[0]))
     paired = experts & (experts - 1) == 0 and shards & (shards - 1) == 0
     plan = by_tokens if paired and 2 * capacity >= rows else by_slots

time: 85.8 us -> 85.3 us (level)
  other arithmetic: 9.39 us -> 8 us
    convert_element_type x3 -> x5, other arithmetic: 2.13 us -> 0.78 us  [the longest x1 0.76 us: pair_targets(): spares = partner.astype(jnp.float32)[:, None]]
    unnamed x20 -> x22, local copies, waits for them, and re-layouts: 3.4 us -> 3.28 us
  transfers between devices with their start and end apart: 21 -> 21, of which waited for: 7 -> 7; matrix products, arithmetic and copies ran while one was open for 39% -> 40% of each run, Pallas kernels for 0% -> 0%
where the time goes in v5:
time: 85.3 us; the launch traced here: 84.8 us
  matrix products  28.4 us (33%)
  waiting for transfers between devices  22.4 us (26%)
  starting transfers between devices  20.8 us (24%)
  other arithmetic  8 us (9%)
  local copies, waits for them, and re-layouts  4.56 us (5%)
    dot_general x21, matrix products, dot32(): return jnp.dot(a, b, preferred_element_type=jnp.float32)  25.1 us
    ppermute x21, waiting for transfers between devices, swap(): return lax.ppermute(value, axis, [(i, i ^ bit) for i in range(count)])  22.4 us
    ppermute x21, starting transfers between devices, swap(): return lax.ppermute(value, axis, [(i, i ^ bit) for i in range(count)])  20.8 us
    unnamed x22, local copies, waits for them, and re-layouts  3.28 us
    dot_general x8, matrix products, by_tokens(): lax.dot_general(pick[r][:, lower:upper], served[r], (((0,), (0,)), ((), (...  3.28 us
  transfers between devices with their start and end apart: 21, of which 7 were waited for; matrix products, arithmetic and copies ran while one was open for 40% of the time, Pallas kernels for 0%

profile of v5, /device:TPU:0, one launch (start us, length us, event | category | flops | bytes accessed | tf_op | source)
XLA Modules:
  0.0 84.8 jit_solution(9642012483774214935)
XLA Ops:
  3.2 2.9 %collective-permute-start.3 = (f32[4,256]{1,0:T(4,128)S(1)}, f32[4,256]{1,0:T(4,128)S(1)}, u32[]{:S(2)}, u32[]{:S(2)}) collective-permute-start(f32[4,256]{1,0:T(4,128)S(1)} %pad_maximum_fusion.30), channel_id=1, source_target_pairs={{0,8},{4,12},{8,0},{12,4},{1,9},{5,13},{9,1},{13,5},{2,10},{6,14},... | collective-permute-start | bytes 12296 | tf_op jit(solution)/shard_map/ppermute | solution.py:43
  6.2 1.4 %convert_reduce_fusion = f32[256]{0:T(256)S(1)} fusion(bf16[256,2048]{1,0:T(8,128)(2,1)} %param.11), kind=kLoop, calls=%fused_computation.29 | loop fusion | flops 1048320 | bytes 1049600 | tf_op jit(solution)/shard_map/reduce_sum | solution.py:29
  7.6 1.6 %fusion.50 = f32[256]{0:T(256)S(1)} fusion(bf16[256,2048]{1,0:T(8,128)(2,1)} %param.11, f32[256]{0:T(256)S(1)} %broadcast_multiply_fusion), kind=kLoop, calls=%fused_computation.48 | loop fusion | flops 2096896 | bytes 1050624 | tf_op jit(solution)/shard_map/reduce_sum | solution.py:31
  15.1 1.5 %convolution_convert_fusion.8 = bf16[128,2048]{1,0:T(8,128)(2,1)S(1)} fusion(bf16[256,2048]{1,0:T(8,128)(2,1)} %collective-permute-done.1, pred[256,256]{1,0:T(32,128)(4,1)S(1)} %fusion.66), kind=kOutput, calls=%fused_computation.44 | convolution fusion | flops 134479872 | bytes 1605632 | tf_op jit(solution)/shard_map/dot_general | solution.py:8
  16.6 3.8 %fusion.18 = f32[256,1024]{1,0:T(8,128)S(1)} fusion(bf16[1,2048,1024]{2,1,0:T(8,128)(2,1)} %param.17, bf16[128,2048]{1,0:T(8,128)(2,1)S(1)} %convolution_convert_fusion.8, bf16[128,2048]{1,0:T(8,128)(2,1)} %convolution_convert_fusion.9), kind=kOutput, calls=%fused_computation.18 | convolution fusion | flops 1075838976 | bytes 6291456 | tf_op jit(solution)/shard_map/dot_general | solution.py:8
  21.7 1.6 %convolution_convert_fusion.6 = bf16[128,2048]{1,0:T(8,128)(2,1)S(1)} fusion(bf16[256,2048]{1,0:T(8,128)(2,1)} %collective-permute-done.1, pred[256,256]{1,0:T(32,128)(4,1)S(1)} %fusion.66), kind=kOutput, calls=%fused_computation.42 | convolution fusion | flops 134479872 | bytes 1605632 | tf_op jit(solution)/shard_map/dot_general | solution.py:8
  25.6 1.3 %fusion.45 = bf16[256,2048]{1,0:T(8,128)(2,1)S(1)} fusion(bf16[1,1024,2048]{2,1,0:T(8,128)(2,1)S(1)} %copy-done.9, f32[256]{0:T(256)S(1)} %bitcast.139, f32[256,1024]{1,0:T(8,128)S(1)} %fusion.18, f32[256,1024]{1,0:T(8,128)S(1)} %fusion.22), kind=kOutput, calls=%fused_computation.33 | convolution fusion | flops 1076363264 | bytes 7341056 | tf_op jit(solution)/shard_map/dot_general | solution.py:8
  30.0 1.3 %fusion.39 = bf16[256,2048]{1,0:T(8,128)(2,1)S(1)} fusion(bf16[1,1024,2048]{2,1,0:T(8,128)(2,1)S(1)} %copy-done.10, f32[256]{0:T(256)S(1)} %bitcast.138, f32[256,1024]{1,0:T(8,128)S(1)} %fusion.6, f32[256,1024]{1,0:T(8,128)S(1)} %fusion.10), kind=kOutput, calls=%fused_computation.31 | convolution fusion | flops 1076363264 | bytes 7341056 | tf_op jit(solution)/shard_map/dot_general | solution.py:8
  31.3 4.1 %collective-permute-done.4 = bf16[256,2048]{1,0:T(8,128)(2,1)S(1)} collective-permute-done((bf16[256,2048]{1,0:T(8,128)(2,1)S(1)}, bf16[256,2048]{1,0:T(8,128)(2,1)S(1)}, u32[]{:S(2)}, u32[]{:S(2)}) %collective-permute-start.4) | collective-permute-done | bytes 1048608 | tf_op jit(solution)/shard_map/ppermute | solution.py:43
  39.1 1.5 %fusion.16 = f32[256,1024]{1,0:T(8,128)S(1)} fusion(bf16[1,2048,1024]{2,1,0:T(8,128)(2,1)S(1)} %copy-done.5, bf16[128,2048]{1,0:T(8,128)(2,1)S(1)} %convolution_convert_fusion.4, bf16[128,2048]{1,0:T(8,128)(2,1)S(1)} %convolution_convert_fusion.5), kind=kOutput, calls=%fused_computation.16 | convolution fusion | flops 1075838976 | bytes 6291456 | tf_op jit(solution)/shard_map/dot_general | solution.py:8
  40.6 1.3 %fusion.20 = f32[256,1024]{1,0:T(8,128)S(1)} fusion(bf16[1,2048,1024]{2,1,0:T(8,128)(2,1)S(1)} %copy-done.6, bf16[128,2048]{1,0:T(8,128)(2,1)S(1)} %convolution_convert_fusion.4, bf16[128,2048]{1,0:T(8,128)(2,1)S(1)} %convolution_convert_fusion.5), kind=kOutput, calls=%fused_computation.20 | convolution fusion | flops 1075838976 | bytes 6291456 | tf_op jit(solution)/shard_map/dot_general | solution.py:8
  43.5 1.3 %fusion.8 = f32[256,1024]{1,0:T(8,128)S(1)} fusion(bf16[1,2048,1024]{2,1,0:T(8,128)(2,1)S(1)} %copy-done.8, bf16[128,2048]{1,0:T(8,128)(2,1)S(1)} %convolution_convert_fusion.2, bf16[128,2048]{1,0:T(8,128)(2,1)S(1)} %convolution_convert_fusion.3), kind=kOutput, calls=%fused_computation.8 | convolution fusion | flops 1075838976 | bytes 6291456 | tf_op jit(solution)/shard_map/dot_general | solution.py:8
  44.8 1.3 %fusion.42 = bf16[256,2048]{1,0:T(8,128)(2,1)S(1)} fusion(bf16[1,1024,2048]{2,1,0:T(8,128)(2,1)S(1)} %copy-done.9, f32[256]{0:T(256)S(1)} %bitcast.137, f32[256,1024]{1,0:T(8,128)S(1)} %fusion.16, f32[256,1024]{1,0:T(8,128)S(1)} %fusion.20), kind=kOutput, calls=%fused_computation.32 | convolution fusion | flops 1076363264 | bytes 7341056 | tf_op jit(solution)/shard_map/dot_general | solution.py:8
  46.2 1.3 %fusion.36 = bf16[256,2048]{1,0:T(8,128)(2,1)S(1)} fusion(bf16[1,1024,2048]{2,1,0:T(8,128)(2,1)S(1)} %copy-done.10, f32[256]{0:T(256)S(1)} %bitcast.136, f32[256,1024]{1,0:T(8,128)S(1)} %fusion.4, f32[256,1024]{1,0:T(8,128)S(1)} %fusion.8), kind=kOutput, calls=%fused_computation.30 | convolution fusion | flops 1076363264 | bytes 7341056 | tf_op jit(solution)/shard_map/dot_general | solution.py:8
  50.0 1.7 %collective-permute-start.13 = (bf16[96,512]{1,0:T(8,128)(2,1)S(1)}, bf16[96,512]{1,0:T(8,128)(2,1)S(1)}, u32[]{:S(2)}, u32[]{:S(2)}) collective-permute-start(bf16[96,512]{1,0:T(8,128)(2,1)S(1)} %get-tuple-element.35), channel_id=1, source_target_pairs={{0,1},{1,0},{2,3},{3,2},{4,5},{5,4},{6,7},{7,6},{8,9},{9,8},{10,11... | collective-permute-start | bytes 294920 | tf_op jit(solution)/shard_map/ppermute | solution.py:43
  53.3 1.9 %collective-permute-start.18 = (bf16[96,512]{1,0:T(8,128)(2,1)S(1)}, bf16[96,512]{1,0:T(8,128)(2,1)S(1)}, u32[]{:S(2)}, u32[]{:S(2)}) collective-permute-start(bf16[96,512]{1,0:T(8,128)(2,1)S(1)} %get-tuple-element.38), channel_id=1, source_target_pairs={{0,1},{1,0},{2,3},{3,2},{4,5},{5,4},{6,7},{7,6},{8,9},{9,8},{10,11... | collective-permute-start | bytes 294920 | tf_op jit(solution)/shard_map/ppermute | solution.py:43
  55.2 2.5 %collective-permute-done.14 = bf16[96,512]{1,0:T(8,128)(2,1)S(1)} collective-permute-done((bf16[96,512]{1,0:T(8,128)(2,1)S(1)}, bf16[96,512]{1,0:T(8,128)(2,1)S(1)}, u32[]{:S(2)}, u32[]{:S(2)}) %collective-permute-start.14) | collective-permute-done | bytes 98336 | tf_op jit(solution)/shard_map/ppermute | solution.py:43
  57.7 2.7 %collective-permute-start.15 = (bf16[96,512]{1,0:T(8,128)(2,1)S(1)}, bf16[96,512]{1,0:T(8,128)(2,1)S(1)}, u32[]{:S(2)}, u32[]{:S(2)}) collective-permute-start(bf16[96,512]{1,0:T(8,128)(2,1)S(1)} %add_convert_fusion.4), channel_id=1, source_target_pairs={{0,2},{1,3},{2,0},{3,1},{4,6},{5,7},{6,4},{7,5},{8,10},{9,11},{10,... | collective-permute-start | bytes 294920 | tf_op jit(solution)/shard_map/ppermute | solution.py:43
  60.4 1.7 %collective-permute-start.17 = (bf16[96,512]{1,0:T(8,128)(2,1)S(1)}, bf16[96,512]{1,0:T(8,128)(2,1)S(1)}, u32[]{:S(2)}, u32[]{:S(2)}) collective-permute-start(bf16[96,512]{1,0:T(8,128)(2,1)S(1)} %get-tuple-element.37), channel_id=1, source_target_pairs={{0,1},{1,0},{2,3},{3,2},{4,5},{5,4},{6,7},{7,6},{8,9},{9,8},{10,11... | collective-permute-start | bytes 294920 | tf_op jit(solution)/shard_map/ppermute | solution.py:43
  63.3 5.4 %collective-permute-done.8 = bf16[160,2048]{1,0:T(8,128)(2,1)S(1)} collective-permute-done((bf16[160,2048]{1,0:T(8,128)(2,1)S(1)}, bf16[160,2048]{1,0:T(8,128)(2,1)S(1)}, u32[]{:S(2)}, u32[]{:S(2)}) %collective-permute-start.8) | collective-permute-done | bytes 655392 | tf_op jit(solution)/shard_map/ppermute | solution.py:43
  69.0 1.7 %collective-permute-start.10 = (bf16[160,512]{1,0:T(8,128)(2,1)S(1)}, bf16[160,512]{1,0:T(8,128)(2,1)S(1)}, u32[]{:S(2)}, u32[]{:S(2)}) collective-permute-start(bf16[160,512]{1,0:T(8,128)(2,1)S(1)} %get-tuple-element.26), channel_id=1, source_target_pairs={{0,1},{1,0},{2,3},{3,2},{4,5},{5,4},{6,7},{7,6},{8,9},{9,8},{10,11... | collective-permute-start | bytes 491528 | tf_op jit(solution)/shard_map/ppermute | solution.py:43
  71.7 3.8 %collective-permute-done.10 = bf16[160,512]{1,0:T(8,128)(2,1)S(1)} collective-permute-done((bf16[160,512]{1,0:T(8,128)(2,1)S(1)}, bf16[160,512]{1,0:T(8,128)(2,1)S(1)}, u32[]{:S(2)}, u32[]{:S(2)}) %collective-permute-start.10) | collective-permute-done | bytes 163872 | tf_op jit(solution)/shard_map/ppermute | solution.py:43
  75.5 3.4 %collective-permute-start.11 = (bf16[160,512]{1,0:T(8,128)(2,1)S(1)}, bf16[160,512]{1,0:T(8,128)(2,1)S(1)}, u32[]{:S(2)}, u32[]{:S(2)}) collective-permute-start(bf16[160,512]{1,0:T(8,128)(2,1)S(1)} %add_convert_fusion.1), channel_id=1, source_target_pairs={{0,2},{1,3},{2,0},{3,1},{4,6},{5,7},{6,4},{7,5},{8,10},{9,11},{10,... | collective-permute-start | bytes 491528 | tf_op jit(solution)/shard_map/ppermute | solution.py:43
  79.0 5.0 %collective-permute-done.11 = bf16[160,512]{1,0:T(8,128)(2,1)S(1)} collective-permute-done((bf16[160,512]{1,0:T(8,128)(2,1)S(1)}, bf16[160,512]{1,0:T(8,128)(2,1)S(1)}, u32[]{:S(2)}, u32[]{:S(2)}) %collective-permute-start.11) | collective-permute-done | bytes 163872 | tf_op jit(solution)/shard_map/ppermute | solution.py:43
  (131 shorter events, 28.1 us)
Async XLA Ops:
  0.0 9.3 %copy-start = (bf16[256,2048]{1,0:T(8,128)(2,1)S(1)}, bf16[256,2048]{1,0:T(8,128)(2,1)}, u32[]{:S(2)}) copy-start(bf16[256,2048]{1,0:T(8,128)(2,1)} %param.11) | copy-start | bytes 3145732
  0.0 9.3 %copy-start.3 = (f32[1,6144]{1,0:T(1,128)S(1)}, f32[1,6144]{1,0:T(1,128)}, u32[]{:S(2)}) copy-start(f32[1,6144]{1,0:T(1,128)} %param.14) | copy-start | bytes 73732
  3.2 7.2 %copy-start.4 = (f32[256,2]{0,1:T(2,128)S(1)}, f32[256,2]{0,1:T(2,128)}, u32[]{:S(2)}) copy-start(f32[256,2]{0,1:T(2,128)} %param.13) | copy-start | bytes 6148
  3.2 9.7 %collective-permute-start.3 = (f32[4,256]{1,0:T(4,128)S(1)}, f32[4,256]{1,0:T(4,128)S(1)}, u32[]{:S(2)}, u32[]{:S(2)}) collective-permute-start(f32[4,256]{1,0:T(4,128)S(1)} %pad_maximum_fusion.30), channel_id=1, source_target_pairs={{0,8},{4,12},{8,0},{12,4},{1,9},{5,13},{9,1},{13,5},{2,10},{6,14},... | collective-permute-start | bytes 12296 | tf_op jit(solution)/shard_map/ppermute | solution.py:43
  6.2 7.1 %collective-permute-start = (f32[4,256]{1,0:T(4,128)S(1)}, f32[4,256]{1,0:T(4,128)S(1)}, u32[]{:S(2)}, u32[]{:S(2)}) collective-permute-start(f32[4,256]{1,0:T(4,128)S(1)} %pad_maximum_fusion.30), channel_id=1, source_target_pairs={{0,4},{4,0},{8,12},{12,8},{1,5},{5,1},{9,13},{13,9},{2,6},{6,2},{1... | collective-permute-start | bytes 12296 | tf_op jit(solution)/shard_map/ppermute | solution.py:43
  9.8 25.6 %collective-permute-start.4 = (bf16[256,2048]{1,0:T(8,128)(2,1)S(1)}, bf16[256,2048]{1,0:T(8,128)(2,1)S(1)}, u32[]{:S(2)}, u32[]{:S(2)}) collective-permute-start(bf16[256,2048]{1,0:T(8,128)(2,1)S(1)} %fusion.53), channel_id=1, source_target_pairs={{0,8},{4,12},{8,0},{12,4},{1,9},{5,13},{9,1},{13,5},{2,10},{6,14},... | collective-permute-start | bytes 3145736 | tf_op jit(solution)/shard_map/ppermute | solution.py:43
  9.9 5.1 %collective-permute-start.1 = (bf16[256,2048]{1,0:T(8,128)(2,1)S(1)}, bf16[256,2048]{1,0:T(8,128)(2,1)}, u32[]{:S(2)}, u32[]{:S(2)}) collective-permute-start(bf16[256,2048]{1,0:T(8,128)(2,1)S(1)} %fusion.53), channel_id=1, source_target_pairs={{0,4},{4,0},{8,12},{12,8},{1,5},{5,1},{9,13},{13,9},{2,6},{6,2},{1... | collective-permute-start | bytes 3145736 | tf_op jit(solution)/shard_map/ppermute | solution.py:43
  13.5 1.2 %collective-permute-start.5 = (f32[4,256]{1,0:T(4,128)S(1)}, f32[4,256]{1,0:T(4,128)S(1)}, u32[]{:S(2)}, u32[]{:S(2)}) collective-permute-start(f32[4,256]{1,0:T(4,128)S(1)} %collective-permute-done.3), channel_id=1, source_target_pairs={{0,4},{4,0},{8,12},{12,8},{1,5},{5,1},{9,13},{13,9},{2,6},{6,2},{1... | collective-permute-start | bytes 12296 | tf_op jit(solution)/shard_map/ppermute | solution.py:43
  35.4 2.7 %collective-permute-start.6 = (bf16[256,2048]{1,0:T(8,128)(2,1)S(1)}, bf16[256,2048]{1,0:T(8,128)(2,1)S(1)}, u32[]{:S(2)}, u32[]{:S(2)}) collective-permute-start(bf16[256,2048]{1,0:T(8,128)(2,1)S(1)} %collective-permute-done.4), channel_id=1, source_target_pairs={{0,4},{4,0},{8,12},{12,8},{1,5},{5,1},{9,13},{13,9},{2,6},{6,2},{1... | collective-permute-start | bytes 3145736 | tf_op jit(solution)/shard_map/ppermute | solution.py:43
  35.9 13.6 %collective-permute-start.12 = (bf16[96,2048]{1,0:T(8,128)(2,1)S(1)}, bf16[96,2048]{1,0:T(8,128)(2,1)S(1)}, u32[]{:S(2)}, u32[]{:S(2)}) collective-permute-start(bf16[96,2048]{1,0:T(8,128)(2,1)S(1)} %convolution_convert_fusion.11), channel_id=1, source_target_pairs={{0,4},{4,0},{8,12},{12,8},{1,5},{5,1},{9,13},{13,9},{2,6},{6,2},{1... | collective-permute-start | bytes 1179656 | tf_op jit(solution)/shard_map/ppermute | solution.py:43
  36.9 25.2 %collective-permute-start.2 = (bf16[160,2048]{1,0:T(8,128)(2,1)S(1)}, bf16[160,2048]{1,0:T(8,128)(2,1)S(1)}, u32[]{:S(2)}, u32[]{:S(2)}) collective-permute-start(bf16[160,2048]{1,0:T(8,128)(2,1)S(1)} %convolution_convert_fusion.1), channel_id=1, source_target_pairs={{0,4},{4,0},{8,12},{12,8},{1,5},{5,1},{9,13},{13,9},{2,6},{6,2},{1... | collective-permute-start | bytes 1966088 | tf_op jit(solution)/shard_map/ppermute | solution.py:43
  48.1 4.0 %collective-permute-start.7 = (bf16[160,2048]{1,0:T(8,128)(2,1)S(1)}, bf16[160,2048]{1,0:T(8,128)(2,1)S(1)}, u32[]{:S(2)}, u32[]{:S(2)}) collective-permute-start(bf16[160,2048]{1,0:T(8,128)(2,1)S(1)} %convolution_convert_fusion), channel_id=1, source_target_pairs={{0,4},{4,0},{8,12},{12,8},{1,5},{5,1},{9,13},{13,9},{2,6},{6,2},{1... | collective-permute-start | bytes 1966088 | tf_op jit(solution)/shard_map/ppermute | solution.py:43
  49.0 3.9 %collective-permute-start.16 = (bf16[96,2048]{1,0:T(8,128)(2,1)S(1)}, bf16[96,2048]{1,0:T(8,128)(2,1)S(1)}, u32[]{:S(2)}, u32[]{:S(2)}) collective-permute-start(bf16[96,2048]{1,0:T(8,128)(2,1)S(1)} %convolution_convert_fusion.10), channel_id=1, source_target_pairs={{0,4},{4,0},{8,12},{12,8},{1,5},{5,1},{9,13},{13,9},{2,6},{6,2},{1... | collective-permute-start | bytes 1179656 | tf_op jit(solution)/shard_map/ppermute | solution.py:43
  50.0 28.9 %collective-permute-start.13 = (bf16[96,512]{1,0:T(8,128)(2,1)S(1)}, bf16[96,512]{1,0:T(8,128)(2,1)S(1)}, u32[]{:S(2)}, u32[]{:S(2)}) collective-permute-start(bf16[96,512]{1,0:T(8,128)(2,1)S(1)} %get-tuple-element.35), channel_id=1, source_target_pairs={{0,1},{1,0},{2,3},{3,2},{4,5},{5,4},{6,7},{7,6},{8,9},{9,8},{10,11... | collective-permute-start | bytes 294920 | tf_op jit(solution)/shard_map/ppermute | solution.py:43
  51.6 6.0 %collective-permute-start.14 = (bf16[96,512]{1,0:T(8,128)(2,1)S(1)}, bf16[96,512]{1,0:T(8,128)(2,1)S(1)}, u32[]{:S(2)}, u32[]{:S(2)}) collective-permute-start(bf16[96,512]{1,0:T(8,128)(2,1)S(1)} %get-tuple-element.36), channel_id=1, source_target_pairs={{0,1},{1,0},{2,3},{3,2},{4,5},{5,4},{6,7},{7,6},{8,9},{9,8},{10,11... | collective-permute-start | bytes 294920 | tf_op jit(solution)/shard_map/ppermute | solution.py:43
  52.5 16.2 %collective-permute-start.8 = (bf16[160,2048]{1,0:T(8,128)(2,1)S(1)}, bf16[160,2048]{1,0:T(8,128)(2,1)S(1)}, u32[]{:S(2)}, u32[]{:S(2)}) collective-permute-start(bf16[160,2048]{1,0:T(8,128)(2,1)S(1)} %add_convert_fusion), channel_id=1, source_target_pairs={{0,8},{4,12},{8,0},{12,4},{1,9},{5,13},{9,1},{13,5},{2,10},{6,14},... | collective-permute-start | bytes 1966088 | tf_op jit(solution)/shard_map/ppermute | solution.py:43
  53.3 7.1 %collective-permute-start.18 = (bf16[96,512]{1,0:T(8,128)(2,1)S(1)}, bf16[96,512]{1,0:T(8,128)(2,1)S(1)}, u32[]{:S(2)}, u32[]{:S(2)}) collective-permute-start(bf16[96,512]{1,0:T(8,128)(2,1)S(1)} %get-tuple-element.38), channel_id=1, source_target_pairs={{0,1},{1,0},{2,3},{3,2},{4,5},{5,4},{6,7},{7,6},{8,9},{9,8},{10,11... | collective-permute-start | bytes 294920 | tf_op jit(solution)/shard_map/ppermute | solution.py:43
  57.7 21.2 %collective-permute-start.15 = (bf16[96,512]{1,0:T(8,128)(2,1)S(1)}, bf16[96,512]{1,0:T(8,128)(2,1)S(1)}, u32[]{:S(2)}, u32[]{:S(2)}) collective-permute-start(bf16[96,512]{1,0:T(8,128)(2,1)S(1)} %add_convert_fusion.4), channel_id=1, source_target_pairs={{0,2},{1,3},{2,0},{3,1},{4,6},{5,7},{6,4},{7,5},{8,10},{9,11},{10,... | collective-permute-start | bytes 294920 | tf_op jit(solution)/shard_map/ppermute | solution.py:43
  60.4 10.3 %collective-permute-start.17 = (bf16[96,512]{1,0:T(8,128)(2,1)S(1)}, bf16[96,512]{1,0:T(8,128)(2,1)S(1)}, u32[]{:S(2)}, u32[]{:S(2)}) collective-permute-start(bf16[96,512]{1,0:T(8,128)(2,1)S(1)} %get-tuple-element.37), channel_id=1, source_target_pairs={{0,1},{1,0},{2,3},{3,2},{4,5},{5,4},{6,7},{7,6},{8,9},{9,8},{10,11... | collective-permute-start | bytes 294920 | tf_op jit(solution)/shard_map/ppermute | solution.py:43
  62.1 8.5 %collective-permute-start.19 = (bf16[96,512]{1,0:T(8,128)(2,1)S(1)}, bf16[96,512]{1,0:T(8,128)(2,1)S(1)}, u32[]{:S(2)}, u32[]{:S(2)}) collective-permute-start(bf16[96,512]{1,0:T(8,128)(2,1)S(1)} %add_convert_fusion.3), channel_id=1, source_target_pairs={{0,2},{1,3},{2,0},{3,1},{4,6},{5,7},{6,4},{7,5},{8,10},{9,11},{10,... | collective-permute-start | bytes 294920 | tf_op jit(solution)/shard_map/ppermute | solution.py:43
  69.0 6.5 %collective-permute-start.10 = (bf16[160,512]{1,0:T(8,128)(2,1)S(1)}, bf16[160,512]{1,0:T(8,128)(2,1)S(1)}, u32[]{:S(2)}, u32[]{:S(2)}) collective-permute-start(bf16[160,512]{1,0:T(8,128)(2,1)S(1)} %get-tuple-element.26), channel_id=1, source_target_pairs={{0,1},{1,0},{2,3},{3,2},{4,5},{5,4},{6,7},{7,6},{8,9},{9,8},{10,11... | collective-permute-start | bytes 491528 | tf_op jit(solution)/shard_map/ppermute | solution.py:43
  70.7 8.2 %collective-permute-start.20 = (bf16[96,512]{1,0:T(8,128)(2,1)S(1)}, bf16[96,512]{1,0:T(8,128)(2,1)S(1)}, u32[]{:S(2)}, u32[]{:S(2)}) collective-permute-start(bf16[96,512]{1,0:T(8,128)(2,1)S(1)} %add_convert_fusion.2), channel_id=1, source_target_pairs={{0,8},{4,12},{8,0},{12,4},{1,9},{5,13},{9,1},{13,5},{2,10},{6,14},... | collective-permute-start | bytes 294920 | tf_op jit(solution)/shard_map/ppermute | solution.py:43
  71.3 7.7 %collective-permute-start.9 = (bf16[160,512]{1,0:T(8,128)(2,1)S(1)}, bf16[160,512]{1,0:T(8,128)(2,1)S(1)}, u32[]{:S(2)}, u32[]{:S(2)}) collective-permute-start(bf16[160,512]{1,0:T(8,128)(2,1)S(1)} %get-tuple-element.25), channel_id=1, source_target_pairs={{0,1},{1,0},{2,3},{3,2},{4,5},{5,4},{6,7},{7,6},{8,9},{9,8},{10,11... | collective-permute-start | bytes 491528 | tf_op jit(solution)/shard_map/ppermute | solution.py:43
  75.5 8.4 %collective-permute-start.11 = (bf16[160,512]{1,0:T(8,128)(2,1)S(1)}, bf16[160,512]{1,0:T(8,128)(2,1)S(1)}, u32[]{:S(2)}, u32[]{:S(2)}) collective-permute-start(bf16[160,512]{1,0:T(8,128)(2,1)S(1)} %add_convert_fusion.1), channel_id=1, source_target_pairs={{0,2},{1,3},{2,0},{3,1},{4,6},{5,7},{6,4},{7,5},{8,10},{9,11},{10,... | collective-permute-start | bytes 491528 | tf_op jit(solution)/shard_map/ppermute | solution.py:43
  (8 other events, 22.3 us)
